TPU v7x, 32 devices: a whole 2x2x4 slice. The times are simulated.
32 devices in a mesh: row: 8 (over z, y), col: 4 (over x, core).
Axes of the slice: x: 2, y: 2, z: 4, core: 2. Of those that a mesh axis runs over, the one named last changes fastest.
Arguments:
- matrix: float32 [18432, 18432], P('row', 'col'), as said below
Outputs:
- updated: float32 [18432, 18432], P('row', 'col')
- reflectors: float32 [18432, 512], P('row')
Inputs may be any that keep to these rules, and one draw needn't show every extreme that they name: matrix is symmetric.
All inputs are finite; a program needn't handle non-finite values.
Results may differ from a plain program's by a relative error of at most 0.00016.
Values sent between devices are 32-bit elements; how exact they have to be, the bound alone decides.
No kernel may reach another device: no remote copies, remote signals or barrier semaphores. Data moves between devices by JAX's collectives and lax.ppermute only.
A program may use at most 256 MiB of HBM per device.

v0:
```python
import jax
import jax.numpy as jnp
from jax import lax
from jax.sharding import PartitionSpec as P

BAND = 256
PANELS = 2


def spread(array, axis, root):
    mine = lax.axis_index(axis) == root
    return lax.psum(jnp.where(mine, array, jnp.zeros_like(array)), axis)


def contract_first(left, right):
    return lax.dot_general(left, right, (((0,), (0,)), ((), ())), precision=lax.Precision.HIGHEST)


def body(matrix):
    high = lax.Precision.HIGHEST
    current = matrix
    row_count = matrix.shape[0]
    col_count = matrix.shape[1]
    row_start = lax.axis_index("row") * row_count
    col_start = lax.axis_index("col") * col_count
    row_places = row_start + jnp.arange(row_count, dtype=jnp.int32)
    col_places = col_start + jnp.arange(col_count, dtype=jnp.int32)
    columns = jnp.arange(BAND, dtype=jnp.int32)
    identity = jnp.eye(BAND, dtype=jnp.float32)
    stored = []
    history = []
    for which_panel in range(PANELS):
        start = (which_panel + 1) * BAND
        low_edge = which_panel * BAND
        high_edge = (which_panel + 1) * BAND
        local_panel = current[:, low_edge:high_edge]
        panel_rows = spread(local_panel, "col", 0)
        row_strip = spread(current[low_edge:high_edge, :], "row", 0)
        panel_rows = jnp.where(row_places[:, None] >= start, panel_rows, 0.0)
        unit_rows = (row_places[:, None] - start == columns[None, :]).astype(jnp.float32)
        gram_sum, top_block = lax.psum(
            (contract_first(panel_rows, panel_rows), contract_first(unit_rows, panel_rows)), "row"
        )
        factor_low = jnp.linalg.cholesky(gram_sum)
        rows_vec_t = (
            jax.scipy.linalg.solve_triangular(factor_low, panel_rows.T, lower=True) + unit_rows.T
        )
        q_top = jax.scipy.linalg.solve_triangular(factor_low, top_block.T, lower=True).T
        shifted = identity + q_top
        factor_two = jnp.linalg.cholesky(jnp.dot(shifted, shifted.T, precision=high))
        inner = jax.scipy.linalg.solve_triangular(factor_two, identity, lower=True)
        transform = jnp.dot(shifted.T, jnp.dot(inner.T, inner, precision=high), precision=high)
        row_strip = jnp.where(col_places[None, :] >= start, row_strip, 0.0)
        unit_cols = (columns[:, None] == col_places[None, :] - start).astype(jnp.float32)
        cols_vec_t = (
            jax.scipy.linalg.solve_triangular(factor_low, row_strip, lower=True) + unit_cols
        )
        stored.append(rows_vec_t)
        image_part = jnp.dot(rows_vec_t, current, precision=high)
        image_cols = lax.psum(image_part, "row")
        curvature = lax.psum(jnp.dot(image_cols, cols_vec_t.T, precision=high), "col")
        row_part = lax.dot_general(cols_vec_t, current, (((1,), (1,)), ((), ())), precision=high)
        image_rows = lax.psum(row_part, "col")
        middle = jnp.dot(jnp.dot(transform, curvature, precision=high), transform.T, precision=high)
        w_cols = jnp.dot(transform, image_cols, precision=high) - 0.5 * jnp.dot(
            middle.T, cols_vec_t, precision=high
        )
        w_rows = jnp.dot(transform, image_rows, precision=high) - 0.5 * jnp.dot(
            middle.T, rows_vec_t, precision=high
        )
        current = current - contract_first(rows_vec_t, w_cols) - contract_first(w_rows, cols_vec_t)
        history.append((rows_vec_t, w_rows, w_cols, cols_vec_t))
    return (current, jnp.concatenate(stored, axis=0).T)


def solution(mesh):
    placed = (P("row", "col"),)
    return jax.shard_map(
        body,
        mesh=mesh,
        in_specs=placed,
        out_specs=(P("row", "col"), P("row", None)),
        check_vma=False,
    )
```

profile of v0, /device:TPU:0, one launch (start us, length us, event | category | flops | bytes accessed | tf_op | source)
XLA Modules:
  0.0 1700.5 jit_solution(7429393631930754318)
XLA Ops:
  15.4 53.9 %all-reduce.14.cloned.1.call-done = f32[2304,256]{1,0:T(8,128)} async-done(((f32[2304,256]{1,0:T(8,128)}), f32[2304,256]{1,0:T(8,128)}) %all-reduce.14.cloned.1.call-update) | async-done | bytes 2359312 | tf_op jit(solution)/shard_map/psum | solution.py:12
  83.3 64.5 %all-reduce.16.cloned.1.call-done = f32[256,256]{0,1:T(8,128)} async-done(((f32[256,256]{0,1:T(8,128)}), f32[256,256]{0,1:T(8,128)}) %all-reduce.16.cloned.1.call-update) | async-done | bytes 262160 | tf_op jit(solution)/shard_map/psum | solution.py:41
  149.9 11.7 cholesky.214
  161.6 9.8 custom-call.25
  172.0 11.9 cholesky.231
  190.2 19.7 %custom-call.26 = f32[2,128,128]{1,2,0:T(8,128)S(1)} custom-call(f32[2,128,128]{2,1,0:T(8,128)S(1)} %get-tuple-element.60), custom_call_target="InvertDiagBlocksLowerTriangular" | custom-call | tf_op jit(solution)/shard_map/jit(_solve_triangular)/triangular_solve | solution.py:46
  216.0 41.5 %fusion.123 = f32[256,4608]{1,0:T(8,128)} fusion(f32[256,2304]{1,0:T(8,128)S(1)} %maximum_add_fusion.2, f32[2304,4608]{1,0:T(8,128)} %param.8), kind=kOutput, calls=%fused_computation.217 | convolution fusion | flops 32614907904 | bytes 49545216 | tf_op jit(solution)/shard_map/dot_general | solution.py:59
  258.1 306.2 %all-reduce.24.cloned.1.call-done = (f32[256,256]{1,0:T(8,128)}, f32[256,4608]{1,0:T(8,128)}, f32[256,4608]{1,0:T(8,128)}) async-done(((f32[256,256]{1,0:T(8,128)}, f32[256,4608]{1,0:T(8,128)}, f32[256,4608]{1,0:T(8,128)}), (f32[256,256]{1,0:T(8,128)}, f32[256,4608]{1,0:T(8,128)}, f32[256,4608]{1,0:T(8,128)})) %all-reduce.24.cloned.1.call-update) | async-done | bytes 9699344 | tf_op jit(solution)/shard_map/psum | solution.py:41
  573.5 41.9 %fusion.32 = f32[256,2304]{1,0:T(8,128)} fusion(f32[2304,4608]{1,0:T(8,128)} %param.8, f32[128,4608]{1,0:T(8,128)S(1)} %fusion.81, f32[128,4608]{1,0:T(8,128)S(1)} %fusion.6, s32[4608]{0:T(1024)S(1)} %fusion.95), kind=kOutput, calls=%fused_computation.77 | convolution fusion | flops 32619626496 | bytes 49563648 | tf_op jit(solution)/shard_map/dot_general | solution.py:62
  623.1 11.7 cholesky.248
  634.9 10.2 custom-call.28
  647.3 11.7 cholesky.265
  667.0 19.7 %custom-call.29 = f32[2,128,128]{1,2,0:T(8,128)S(1)} custom-call(f32[2,128,128]{2,1,0:T(8,128)S(1)} %get-tuple-element.62), custom_call_target="InvertDiagBlocksLowerTriangular" | custom-call | tf_op jit(solution)/shard_map/jit(_solve_triangular)/triangular_solve | solution.py:51
  700.9 47.1 %all-reduce.28.cloned.1.call-done = (f32[256,256]{1,0:T(8,128)}, f32[256,2304]{1,0:T(8,128)}) async-done(((f32[256,256]{1,0:T(8,128)}, f32[256,2304]{1,0:T(8,128)}), (f32[256,256]{1,0:T(8,128)}, f32[256,2304]{1,0:T(8,128)})) %all-reduce.28.cloned.1.call-update) | async-done | bytes 2621456 | tf_op jit(solution)/shard_map/psum | solution.py:61
  761.9 39.0 %fusion.127 = f32[2304,4608]{1,0:T(8,128)} fusion(f32[256,2304]{1,0:T(8,128)S(1)} %copy-done.1, f32[256,4608]{1,0:T(8,128)S(1)} %fusion.1), kind=kOutput, calls=%fused_computation.221 | convolution fusion | flops 32614907904 | bytes 49545216 | tf_op jit(solution)/shard_map/dot_general | solution.py:16
  800.9 51.5 %subtract_subtract_fusion.1 = f32[2304,4608]{1,0:T(8,128)} fusion(f32[2304,4608]{1,0:T(8,128)} %param.8, f32[2304,4608]{1,0:T(8,128)} %fusion.127, f32[256,2304]{1,0:T(8,128)S(1)} %copy-done.14, f32[256,4608]{1,0:T(8,128)} %maximum_add_fusion.15), kind=kOutput, calls=%fused_computation.9 | convolution fusion | flops 32636141568 | bytes 134479872 | tf_op jit(solution)/shard_map/dot_general | solution.py:16
  860.5 51.0 %all-reduce.18.cloned.1.call-done = f32[2304,256]{1,0:T(8,128)} async-done(((f32[2304,256]{1,0:T(8,128)}), f32[2304,256]{1,0:T(8,128)}) %all-reduce.18.cloned.1.call-update) | async-done | bytes 2359312 | tf_op jit(solution)/shard_map/psum | solution.py:12
  925.6 64.4 %all-reduce.20.cloned.1.call-done = f32[256,256]{0,1:T(8,128)} async-done(((f32[256,256]{0,1:T(8,128)}), f32[256,256]{0,1:T(8,128)}) %all-reduce.20.cloned.1.call-update) | async-done | bytes 262160 | tf_op jit(solution)/shard_map/psum | solution.py:41
  992.1 11.7 cholesky.282
  1003.9 9.8 custom-call.31
  1014.2 11.9 cholesky.299
  1033.0 19.7 %custom-call.32 = f32[2,128,128]{1,2,0:T(8,128)S(1)} custom-call(f32[2,128,128]{2,1,0:T(8,128)S(1)} %get-tuple-element.64), custom_call_target="InvertDiagBlocksLowerTriangular" | custom-call | tf_op jit(solution)/shard_map/jit(_solve_triangular)/triangular_solve | solution.py:46
  1058.8 41.5 %fusion.129 = f32[256,4608]{1,0:T(8,128)} fusion(f32[256,2304]{1,0:T(8,128)S(1)} %maximum_add_fusion.3, f32[2304,4608]{1,0:T(8,128)} %subtract_subtract_fusion.1), kind=kOutput, calls=%fused_computation.223 | convolution fusion | flops 32614907904 | bytes 49545216 | tf_op jit(solution)/shard_map/dot_general | solution.py:59
  1113.1 294.0 %all-reduce.22.cloned.1.call-done = (f32[256,256]{1,0:T(8,128)}, f32[256,4608]{1,0:T(8,128)}, f32[256,4608]{1,0:T(8,128)}) async-done(((f32[256,256]{1,0:T(8,128)}, f32[256,4608]{1,0:T(8,128)}, f32[256,4608]{1,0:T(8,128)}), (f32[256,256]{1,0:T(8,128)}, f32[256,4608]{1,0:T(8,128)}, f32[256,4608]{1,0:T(8,128)})) %all-reduce.22.cloned.1.call-update) | async-done | bytes 9699344 | tf_op jit(solution)/shard_map/psum | solution.py:41
  1416.3 42.0 %fusion.30 = f32[256,2304]{1,0:T(8,128)} fusion(f32[2304,4608]{1,0:T(8,128)} %subtract_subtract_fusion.1, f32[128,4608]{1,0:T(8,128)S(1)} %fusion.84, f32[128,4608]{1,0:T(8,128)S(1)} %fusion.4, s32[4608]{0:T(1024)S(1)} %fusion.93), kind=kOutput, calls=%fused_computation.75 | convolution fusion | flops 32619626496 | bytes 49563648 | tf_op jit(solution)/shard_map/dot_general | solution.py:62
  1465.9 11.7 cholesky.316
  1477.7 10.2 custom-call.34
  1490.1 11.7 cholesky.333
  1508.4 19.7 %custom-call.35 = f32[2,128,128]{1,2,0:T(8,128)S(1)} custom-call(f32[2,128,128]{2,1,0:T(8,128)S(1)} %get-tuple-element.66), custom_call_target="InvertDiagBlocksLowerTriangular" | custom-call | tf_op jit(solution)/shard_map/jit(_solve_triangular)/triangular_solve | solution.py:51
  1542.4 46.9 %all-reduce.26.cloned.1.call-done = (f32[256,256]{1,0:T(8,128)}, f32[256,2304]{1,0:T(8,128)}) async-done(((f32[256,256]{1,0:T(8,128)}, f32[256,2304]{1,0:T(8,128)}), (f32[256,256]{1,0:T(8,128)}, f32[256,2304]{1,0:T(8,128)})) %all-reduce.26.cloned.1.call-update) | async-done | bytes 2621456 | tf_op jit(solution)/shard_map/psum | solution.py:61
  1603.2 38.8 %fusion.133 = f32[2304,4608]{1,0:T(8,128)} fusion(f32[256,2304]{1,0:T(8,128)S(1)} %copy-done.4, f32[256,4608]{1,0:T(8,128)S(1)} %fusion), kind=kOutput, calls=%fused_computation.227 | convolution fusion | flops 32614907904 | bytes 49545216 | tf_op jit(solution)/shard_map/dot_general | solution.py:16
  1642.0 51.4 %subtract_subtract_fusion = f32[2304,4608]{1,0:T(8,128)} fusion(f32[2304,4608]{1,0:T(8,128)} %subtract_subtract_fusion.1, f32[2304,4608]{1,0:T(8,128)} %fusion.133, f32[256,2304]{1,0:T(8,128)S(1)} %copy-done.13, f32[256,4608]{1,0:T(8,128)} %maximum_add_fusion.14), kind=kOutput, calls=%fused_computation.8 | convolution fusion | flops 32636141568 | bytes 134479872 | tf_op jit(solution)/shard_map/dot_general | solution.py:16
  (234 shorter events, 208.8 us)
Async XLA Ops:
  7.2 62.1 %all-reduce.14.cloned.1.call-start = ((), (), s32[]{:S(2)}) async-start(), calls=%async_computation | async-start | bytes 4718592 | tf_op jit(solution)/shard_map/psum | solution.py:12
  10.5 137.3 %all-reduce.16.cloned.1.call-start = ((), (), s32[]{:S(2)}) async-start(), calls=%async_computation.1 | async-start | bytes 524288 | tf_op jit(solution)/shard_map/psum | solution.py:41
  77.0 487.3 %all-reduce.24.cloned.1.call-start = ((), (), s32[]{:S(2)}) async-start(), calls=%async_computation.5 | async-start | bytes 19398656 | tf_op jit(solution)/shard_map/psum | solution.py:41
  190.2 22.9 %copy-start.27 = (s32[2,2]{1,0:T(2,128)}, s32[2,2]{1,0:T(2,128)S(1)}, u32[]{:S(2)}) copy-start(s32[2,2]{1,0:T(2,128)S(1)} %get-tuple-element.390) | copy-start | bytes 52
  257.5 490.5 %all-reduce.28.cloned.1.call-start = ((), (), s32[]{:S(2)}) async-start(), calls=%async_computation.7 | async-start | bytes 5242880 | tf_op jit(solution)/shard_map/psum | solution.py:61
  258.1 357.4 %copy-start.21 = (s32[4608]{0:T(1024)}, s32[4608]{0:T(1024)S(1)}, u32[]{:S(2)}) copy-start(s32[4608]{0:T(1024)S(1)} %fusion.95) | copy-start | bytes 55300
  571.3 44.1 %slice-start = ((s8[4718592]{0:T(1024)(128)(4,1)}), s8[4194304]{0:T(1024)(128)(4,1)S(1)}, s32[]{:S(2)}) async-start(s8[4718592]{0:T(1024)(128)(4,1)} %bitcast.219), calls=%async_computation.8 | async-start | bytes 8388608
  573.5 41.9 %copy-start.8 = (f32[128,4608]{1,0:T(8,128)}, f32[128,4608]{1,0:T(8,128)S(1)}, u32[]{:S(2)}) copy-start(f32[128,4608]{1,0:T(8,128)S(1)} %fusion.81) | copy-start | bytes 7077892
  573.5 41.9 %slice-start.1 = ((s8[4718592]{0:T(1024)(128)(4,1)}), s8[524288]{0:T(1024)(128)(4,1)S(1)}, s32[]{:S(2)}) async-start(s8[4718592]{0:T(1024)(128)(4,1)} %bitcast.219), calls=%async_computation.9 | async-start | bytes 1048576
  615.5 5.2 copy-start.25
  688.8 9.4 copy-start.22
  688.8 222.8 %all-reduce.18.cloned.1.call-start = ((), (), s32[]{:S(2)}) async-start(), calls=%async_computation.2 | async-start | bytes 4718592 | tf_op jit(solution)/shard_map/psum | solution.py:12
  688.8 9.3 copy-start.9
  747.9 4.0 copy-start.23
  747.9 4.8 copy-start.1
  752.8 3.8 copy-start.10
  761.9 39.0 %copy-start.14 = (f32[256,2304]{1,0:T(8,128)S(1)}, f32[256,2304]{1,0:T(8,128)}, u32[]{:S(2)}) copy-start(f32[256,2304]{1,0:T(8,128)} %fusion.3) | copy-start | bytes 7077892
  855.7 134.4 %all-reduce.20.cloned.1.call-start = ((), (), s32[]{:S(2)}) async-start(), calls=%async_computation.3 | async-start | bytes 524288 | tf_op jit(solution)/shard_map/psum | solution.py:41
  919.3 487.8 %all-reduce.22.cloned.1.call-start = ((), (), s32[]{:S(2)}) async-start(), calls=%async_computation.4 | async-start | bytes 19398656 | tf_op jit(solution)/shard_map/psum | solution.py:41
  922.1 106.7 %copy-start.28 = (s32[2,2]{1,0:T(2,128)S(1)}, s32[2,2]{1,0:T(2,128)}, u32[]{:S(2)}) copy-start(s32[2,2]{1,0:T(2,128)} %get-tuple-element.391) | copy-start | bytes 52
  1100.3 489.1 %all-reduce.26.cloned.1.call-start = ((), (), s32[]{:S(2)}) async-start(), calls=%async_computation.6 | async-start | bytes 5242880 | tf_op jit(solution)/shard_map/psum | solution.py:61
  1101.9 356.3 %copy-start.19 = (s32[4608]{0:T(1024)}, s32[4608]{0:T(1024)S(1)}, u32[]{:S(2)}) copy-start(s32[4608]{0:T(1024)S(1)} %fusion.93) | copy-start | bytes 55300
  1414.1 44.2 %slice-start.2 = ((s8[4718592]{0:T(1024)(128)(4,1)}), s8[4194304]{0:T(1024)(128)(4,1)S(1)}, s32[]{:S(2)}) async-start(s8[4718592]{0:T(1024)(128)(4,1)} %bitcast.221), calls=%async_computation.10 | async-start | bytes 8388608
  1416.3 42.0 %copy-start.5 = (f32[128,4608]{1,0:T(8,128)}, f32[128,4608]{1,0:T(8,128)S(1)}, u32[]{:S(2)}) copy-start(f32[128,4608]{1,0:T(8,128)S(1)} %fusion.84) | copy-start | bytes 7077892
  1416.3 42.0 %slice-start.3 = ((s8[4718592]{0:T(1024)(128)(4,1)}), s8[524288]{0:T(1024)(128)(4,1)S(1)}, s32[]{:S(2)}) async-start(s8[4718592]{0:T(1024)(128)(4,1)} %bitcast.221), calls=%async_computation.11 | async-start | bytes 1048576
  1458.3 5.2 copy-start.26
  1463.6 40.9 %copy-start.29 = (s32[2,2]{1,0:T(2,128)S(1)}, s32[2,2]{1,0:T(2,128)}, u32[]{:S(2)}) copy-start(s32[2,2]{1,0:T(2,128)} %get-tuple-element.391) | copy-start | bytes 52
  1530.2 9.4 copy-start.6
  1530.2 9.4 copy-start.20
  1589.4 4.0 copy-start.24
  1589.4 4.8 copy-start.4
  1603.2 38.8 %copy-start.13 = (f32[256,2304]{1,0:T(8,128)S(1)}, f32[256,2304]{1,0:T(8,128)}, u32[]{:S(2)}) copy-start(f32[256,2304]{1,0:T(8,128)} %fusion.2) | copy-start | bytes 7077892
  (10 other events, 22.7 us)
Sparse Core Ops, SparseCore 0:
  10.9 58.3 all-reduce.13
  77.1 70.6 all-reduce.15
  257.6 306.6 all-reduce.23
  688.9 59.0 all-reduce.27
  855.8 55.7 all-reduce.17
  919.4 70.6 all-reduce.19
  1100.4 306.5 all-reduce.21
  1530.3 59.0 all-reduce.25
where the time goes:
time: 1710 us; the launch traced here: 1700 us
  waiting for transfers between devices  928 us (54%)
  matrix products  460 us (27%)
  other arithmetic  258 us (15%)
  local copies, waits for them, and re-layouts  32.3 us (2%)
  between operations  20.8 us (1%)
    psum x4, waiting for transfers between devices, body(): lax.psum((contract_first(panel_rows, panel_rows), contract_first(unit_row...  729 us
    dot_general x8, matrix products, contract_first(): lax.dot_general(left, right, (((0,), (0,)), ((), ())), precision=lax.Prec...  203 us
    psum x2, waiting for transfers between devices, spread(): return lax.psum(jnp.where(mine, array, jnp.zeros_like(array)), axis)  105 us
    psum x2, waiting for transfers between devices, body(): lax.psum(jnp.dot(image_cols, cols_vec_t.T, precision=high), 'col')  94 us
    dot_general x2, matrix products, body(): lax.dot_general(cols_vec_t, current, (((1,), (1,)), ((), ())), precision=...  83.9 us
    dot_general x2, matrix products, body(): image_part = jnp.dot(rows_vec_t, current, precision=high)  82.9 us
    another operation x14, other arithmetic, body(): jnp.linalg.cholesky(jnp.dot(shifted, shifted.T, precision=high))  70 us
    another operation x13, other arithmetic, body(): factor_low = jnp.linalg.cholesky(gram_sum)  69.1 us
  transfers between devices with their start and end apart: 8, of which 8 were waited for; matrix products, arithmetic and copies ran while one was open for 3% of the time, Pallas kernels for 0%

commit v1 on v0

v1 whole, which is shorter than its diff:
```python
import functools

import jax
import jax.numpy as jnp
from jax import lax
from jax.experimental import pallas as pl
from jax.experimental.pallas import tpu as pltpu
from jax.sharding import PartitionSpec as P

BAND = 256
NB = 64
EXACT = lax.Precision.HIGHEST


def dot_in(left, right, dims=((1,), (0,))):
    return lax.dot_general(
        left, right, (dims, ((), ())), precision=EXACT, preferred_element_type=jnp.float32
    )


def beside_identity(block):
    size = block.shape[0]
    rows = lax.broadcasted_iota(jnp.int32, (size, size), 0)
    columns = lax.broadcasted_iota(jnp.int32, (size, size), 1)
    return jnp.concatenate([block, (rows == columns).astype(jnp.float32)], axis=1)


def eliminate_below(both):
    size = both.shape[0]
    tiles = [both[8 * i : 8 * i + 8] for i in range(size // 8)]
    place = lax.broadcasted_iota(jnp.int32, (8, 2 * size), 0)
    for k in range(size):
        first, inside = divmod(k, 8)
        row = tiles[first][inside : inside + 1, :]
        scale = lax.rsqrt(row[:, k : k + 1])
        scaled = row * scale
        twice = scaled * scale
        for b in range(first, len(tiles)):
            new = tiles[b] - tiles[b][:, k : k + 1] * twice
            if b == first:
                new = jnp.where(place > inside, new, jnp.where(place == inside, scaled, tiles[b]))
            tiles[b] = new
    return jnp.concatenate(tiles, axis=0)


def eliminate_all(both):
    size = both.shape[0]
    tiles = [both[8 * i : 8 * i + 8] for i in range(size // 8)]
    place = lax.broadcasted_iota(jnp.int32, (8, 2 * size), 0)
    for k in range(size):
        first, inside = divmod(k, 8)
        row = tiles[first][inside : inside + 1, :]
        scaled = row / row[:, k : k + 1]
        new_tiles = []
        for b in range(len(tiles)):
            new = tiles[b] - tiles[b][:, k : k + 1] * scaled
            if b == first:
                new = jnp.where(place == inside, scaled, new)
            new_tiles.append(new)
        tiles = new_tiles
    return jnp.concatenate(tiles, axis=0)


def square_places():
    rows = lax.broadcasted_iota(jnp.int32, (BAND, BAND), 0)
    columns = lax.broadcasted_iota(jnp.int32, (BAND, BAND), 1)
    return rows, columns


def factor_kernel(at, start_ref, out_ref, *scratch):
    work_ref = scratch[0] if scratch else out_ref
    rows, columns = square_places()
    if at == 0:
        work_ref[:, :BAND] = start_ref[...]
        work_ref[:, BAND:] = (rows == columns).astype(jnp.float32)
    else:
        work_ref[...] = start_ref[...]
    end = at + NB
    both = eliminate_below(beside_identity(work_ref[at:end, at:end]))
    strip = dot_in(both[:, NB:], work_ref[at:end, :])
    work_ref[at:end, :] = strip
    if end < BAND:
        work_ref[end:, :] -= dot_in(strip[:, end:BAND], strip, ((0,), (0,)))
    else:
        out_ref[...] = jnp.where(rows >= columns, work_ref[:, BAND:], 0.0)


def transform_kernel(at, *refs):
    if at == 0:
        top_ref, inverse_ref, out_ref = refs
        rows, columns = square_places()
        identity = (rows == columns).astype(jnp.float32)
        work_ref = out_ref
        work_ref[:, :BAND] = identity + dot_in(top_ref[...], inverse_ref[...], ((1,), (1,)))
        work_ref[:, BAND:] = identity
    else:
        start_ref, out_ref = refs[:2]
        work_ref = refs[2] if len(refs) > 2 else out_ref
        work_ref[...] = start_ref[...]
    end = at + NB
    both = eliminate_all(beside_identity(work_ref[at:end, at:end]))
    strip = dot_in(both[:, NB:], work_ref[at:end, :])
    if at > 0:
        work_ref[:at, :] -= dot_in(work_ref[:at, at:end], strip)
    if end < BAND:
        work_ref[end:, :] -= dot_in(work_ref[end:, at:end], strip)
    work_ref[at:end, :] = strip
    if end == BAND:
        out_ref[...] = work_ref[:, BAND:]


def by_steps(kernel, name, *operands):
    for at in range(0, BAND, NB):
        last = at + NB == BAND
        shape = (BAND, BAND) if last else (BAND, 2 * BAND)
        operands = (
            pl.pallas_call(
                functools.partial(kernel, at),
                out_shape=jax.ShapeDtypeStruct(shape, jnp.float32),
                scratch_shapes=[pltpu.VMEM((BAND, 2 * BAND), jnp.float32)] if last else [],
                cost_estimate=pl.CostEstimate(
                    flops=6 * 10**9, bytes_accessed=4 * 10**6, transcendentals=BAND
                ),
                name=name,
            )(*operands),
        )
    return operands[0]


NN, NT, TN = ((1,), (0,)), ((1,), (1,)), ((0,), (0,))
GRANT = 56 * 2**20


def halves(value):
    high = value.astype(jnp.bfloat16)
    return high, (value - high.astype(jnp.float32)).astype(jnp.bfloat16)


def dot1(left, right, dims):
    return lax.dot_general(left, right, (dims, ((), ())), preferred_element_type=jnp.float32)


def dot3(left, right, dims):
    lh, ll = halves(left)
    rh, rl = halves(right)
    return dot1(lh, rh, dims) + (dot1(lh, rl, dims) + dot1(ll, rh, dims))


def places_of(offset_ref, size):
    at = offset_ref[0] + pl.program_id(0) * size
    return at + lax.broadcasted_iota(jnp.int32, (size, BAND), 0)


def unit_of(places, start):
    columns = lax.broadcasted_iota(jnp.int32, places.shape, 1)
    return (places - start == columns).astype(jnp.float32)


def add_to(ref, value):
    @pl.when(pl.program_id(0) == 0)
    def _():
        ref[...] = value

    @pl.when(pl.program_id(0) > 0)
    def _():
        ref[...] += value


def first_kernel(offset_ref, raw_ref, image_ref, next_ref, inv_ref, y_ref, x_ref, mid_ref):
    places = places_of(offset_ref, raw_ref.shape[0])
    panel = jnp.where(places >= BAND, raw_ref[...], 0.0)
    y = dot3(panel, inv_ref[...], NT) + unit_of(places, BAND)
    x = dot3(image_ref[...], inv_ref[...], NT) + next_ref[...]
    y_ref[...] = y
    x_ref[...] = x
    add_to(mid_ref, dot3(y, x, TN))


def curvature(tm_ref, mid_ref):
    return dot3(dot3(tm_ref[...], mid_ref[...], NN), tm_ref[...], NT)


def second_kernel(
    offset_ref, y_ref, x_ref, next_ref, tm_ref, mid_ref, xh_ref, top_ref, inv_ref, w_ref, panel_ref, wh_ref, gram_ref, inner_ref
):
    places = places_of(offset_ref, y_ref.shape[0])
    s = curvature(tm_ref, mid_ref)
    rows, columns = square_places()
    yh = dot3(top_ref[...], inv_ref[...], NT) + (rows == columns).astype(F32)
    wh = dot3(xh_ref[...], tm_ref[...], NT) - 0.5 * dot3(yh, s, NN)
    y = y_ref[...]
    w = dot3(x_ref[...], tm_ref[...], NT) - 0.5 * dot3(y, s, NN)
    w_ref[...] = w
    panel = next_ref[...] - dot3(y, wh, NT) - dot3(w, yh, NT)
    panel_ref[...] = panel
    wh_ref[...] = wh
    panel = jnp.where(places >= 2 * BAND, panel, 0.0)
    add_to(gram_ref, dot_in(panel, panel, TN))
    add_to(inner_ref, jnp.concatenate([dot3(w, panel, TN), dot3(y, panel, TN)], axis=0))


def vectors_kernel(start, offset_ref, panel_ref, inv_ref, y_ref):
    places = places_of(offset_ref, panel_ref.shape[0])
    panel = jnp.where(places >= start, panel_ref[...], 0.0)
    y_ref[...] = dot3(panel, inv_ref[...], NT) + unit_of(places, start)


def halves_kernel(offset_ref, panel_ref, high_ref, low_ref):
    places = places_of(offset_ref, panel_ref.shape[0])
    high_ref[...], low_ref[...] = halves(jnp.where(places >= 2 * BAND, panel_ref[...], 0.0))


def sides_kernel(offset_ref, raw_ref, next_ref, panel_ref, inv_ref, tm_ref, wh_ref, y_ref, w_ref):
    places = places_of(offset_ref, raw_ref.shape[0])
    raw = jnp.where(places >= BAND, raw_ref[...], 0.0)
    y = dot3(raw, inv_ref[...], NT) + unit_of(places, BAND)
    y_ref[...] = y
    w_ref[...] = dot3(next_ref[...] - panel_ref[...] - dot3(y, wh_ref[...], NT), tm_ref[...], NT)


def last_kernel(y_ref, x_ref, tm_ref, mid_ref, w_ref):
    s = curvature(tm_ref, mid_ref)
    w_ref[...] = dot3(x_ref[...], tm_ref[...], NT) - 0.5 * dot3(y_ref[...], s, NN)


def gram_kernel(offset_ref, raw_ref, gram_ref, high_ref, low_ref):
    panel = jnp.where(places_of(offset_ref, raw_ref.shape[0]) >= BAND, raw_ref[...], 0.0)
    high_ref[...], low_ref[...] = halves(panel)
    add_to(gram_ref, dot_in(panel, panel, TN))


def next_kernel(
    offset_ref, raw_ref, y_ref, w_ref, wn_ref, low_ref, inv_ref, image_ref, inner_ref, panel_ref, new_ref, out_ref, v_ref, mid_ref
):
    y, w = y_ref[...], w_ref[...]
    yn = dot3(low_ref[...], inv_ref[...], NT)
    third = raw_ref[...] - dot3(y, wn_ref[...], NT) - dot3(w, yn, NT)
    image = image_ref[...] - dot3(y, inner_ref[:BAND], NN) - dot3(w, inner_ref[BAND:], NN)
    out = dot3(image, new_ref[...], NT) + third
    places = places_of(offset_ref, y.shape[0])
    panel = jnp.where(places >= 2 * BAND, panel_ref[...], 0.0)
    v = dot3(panel, new_ref[...], NT) + unit_of(places, 2 * BAND)
    out_ref[...] = out
    v_ref[...] = v
    add_to(mid_ref, dot3(v, out, TN))


F32, BF16 = jnp.float32, jnp.bfloat16


def by_rows(kernel, name, rows, operands, outs, flops):
    tile = rows // 4 if rows > 1000 and rows % 64 == 0 else rows

    def spec(shape):
        if shape[0] == rows:
            return pl.BlockSpec((tile, shape[1]), lambda i: (i, 0))
        return pl.BlockSpec(shape, lambda i: (0,) * len(shape))

    in_specs = [
        pl.BlockSpec(memory_space=pltpu.SMEM) if v.dtype == jnp.int32 else spec(v.shape) for v in operands
    ]
    shapes = [
        jax.ShapeDtypeStruct(o, F32) if isinstance(o, tuple) else jax.ShapeDtypeStruct((rows, BAND), o)
        for o in outs
    ]
    return pl.pallas_call(
        kernel,
        grid=(rows // tile,),
        in_specs=in_specs,
        out_specs=[spec(shape.shape) for shape in shapes],
        out_shape=shapes,
        compiler_params=pltpu.CompilerParams(vmem_limit_bytes=GRANT),
        cost_estimate=pl.CostEstimate(
            flops=flops * 12 * rows * BAND * BAND, bytes_accessed=4 * rows * BAND * 6, transcendentals=0
        ),
        name=name,
    )(*operands)


def image_kernel(matrix_ref, high_ref, low_ref, out_ref):
    high_panel = high_ref[...]
    both = jnp.concatenate([high_panel, low_ref[...]], axis=1)
    m = matrix_ref.shape[0]
    step = m // 4

    def part(at):
        high, low = halves(matrix_ref[at : at + step, :])
        wide = dot1(high, both, NN)
        return wide[:, :BAND] + (wide[:, BAND:] + dot1(low, high_panel, NN))

    @pl.when(pl.program_id(0) == 0)
    def _():
        for at in range(0, m, step):
            out_ref[at : at + step, :] = part(at)

    @pl.when(pl.program_id(0) > 0)
    def _():
        for at in range(0, m, step):
            out_ref[at : at + step, :] += part(at)


def image_of(matrix, high, low):
    m, n = matrix.shape
    deep = 512 if n % 512 == 0 else 256
    return pl.pallas_call(
        image_kernel,
        grid=(n // deep,),
        in_specs=[
            pl.BlockSpec((m, deep), lambda i: (0, i)),
            pl.BlockSpec((deep, BAND), lambda i: (i, 0)),
            pl.BlockSpec((deep, BAND), lambda i: (i, 0)),
        ],
        out_specs=pl.BlockSpec((m, BAND), lambda i: (0, 0)),
        out_shape=jax.ShapeDtypeStruct((m, BAND), F32),
        compiler_params=pltpu.CompilerParams(vmem_limit_bytes=GRANT),
        cost_estimate=pl.CostEstimate(
            flops=8 * m * n * BAND, bytes_accessed=4 * m * n, transcendentals=0
        ),
        name="image",
    )(matrix, high, low)


def update_kernel(matrix_ref, yr_ref, wr_ref, yc_ref, wc_ref, *rest):
    out_ref, high_ref, low_ref = rest[-3:]

    @pl.when(pl.program_id(0) == 0)
    def _():
        high_ref[:, :BAND], low_ref[:, :BAND] = halves(yr_ref[...])
        high_ref[:, BAND:], low_ref[:, BAND:] = halves(wr_ref[...])

    rh, rl = halves(jnp.concatenate([wc_ref[...], yc_ref[...]], axis=1))
    m = matrix_ref.shape[0]
    step = m // 4
    for at in range(0, m, step):
        part = slice(at, at + step)
        high, low = high_ref[part, :], low_ref[part, :]
        product = dot1(high, rh, NT) + (dot1(high, rl, NT) + dot1(low, rh, NT))
        out_ref[part, :] = matrix_ref[part, :] - product


def update(matrix, y_r, w_r, y_c, w_c, name, parts=1):
    m, n = matrix.shape
    wide = 512 if n % 512 == 0 else n // 9 if n % (9 * 128) == 0 else n
    blocks = n // wide
    parts = parts if blocks % parts == 0 else 1
    each = blocks // parts
    out = None
    for part in range(parts):
        here = functools.partial(lambda first, i: (0, first + i), part * each)
        down = functools.partial(lambda first, i: (first + i, 0), part * each)
        whole = pl.BlockSpec((m, BAND), lambda i: (0, 0), pipeline_mode=pl.Buffered(1))
        specs = [pl.BlockSpec((m, wide), here), whole, whole]
        specs += [pl.BlockSpec((wide, BAND), down)] * 2
        operands = [matrix, y_r, w_r, y_c, w_c]
        if out is not None:
            specs.append(pl.BlockSpec(memory_space=pl.ANY))
            operands.append(out)
        out = pl.pallas_call(
            update_kernel,
            grid=(each,),
            in_specs=specs,
            out_specs=pl.BlockSpec((m, wide), here),
            out_shape=jax.ShapeDtypeStruct((m, n), F32),
            scratch_shapes=[pltpu.VMEM((m, 2 * BAND), BF16)] * 2,
            input_output_aliases={5: 0} if len(operands) > 5 else {},
            compiler_params=pltpu.CompilerParams(vmem_limit_bytes=GRANT),
            cost_estimate=pl.CostEstimate(
                flops=16 * m * n * BAND // parts, bytes_accessed=8 * m * n // parts, transcendentals=0
            ),
            name=name,
        )(*operands)
    return out


class Moves:
    def __init__(self, mesh):
        self.rows = mesh.shape["row"]
        self.cols = mesh.shape["col"]
        self.per = self.rows // self.cols
        self.row = lax.axis_index("row")
        self.col = lax.axis_index("col")
        self.group = self.row // self.per
        self.lane = self.row % self.per

    def over_col(self, value, to):
        return lax.ppermute(value, "col", [(c, to(c)) for c in range(self.cols) if to(c) is not None])

    def over_both(self, value, pairs):
        flat = [(a * self.cols + b, d * self.cols + e) for (a, b), (d, e) in pairs]
        return lax.ppermute(value, ("row", "col"), flat)

    def spread(self, value):
        bit = self.cols // 2
        while bit:
            got = self.over_col(value, lambda c: c + bit if c % (2 * bit) == 0 else None)
            value = jnp.where(self.col % (2 * bit) == bit, got, value)
            bit //= 2
        return value

    def total(self, value):
        bit = 1
        while bit < self.cols:
            value = value + self.over_col(value, lambda c: c ^ bit)
            bit *= 2
        return value

    def bits(self):
        return [1 << i for i in range(self.cols.bit_length() - 1)]

    def scatter_sum(self, value):
        bits = self.bits()
        value = value.reshape(*[2] * len(bits), value.shape[0] // self.cols, value.shape[1])
        for bit in bits:
            axis = value.ndim - 3
            odd = (self.col // bit) % 2 == 1
            first = lax.index_in_dim(value, 0, axis, keepdims=False)
            second = lax.index_in_dim(value, 1, axis, keepdims=False)
            keep, give = jnp.where(odd, second, first), jnp.where(odd, first, second)
            value = keep + self.over_col(give, lambda c: c ^ bit)
        return value

    def collect(self, piece):
        for bit in self.bits()[::-1]:
            other = self.over_col(piece, lambda c: c ^ bit)
            odd = (self.col // bit) % 2 == 1
            piece = jnp.stack([jnp.where(odd, other, piece), jnp.where(odd, piece, other)], axis=-3)
        return piece.reshape(-1, piece.shape[-1])

    def over_row(self, value, to):
        return lax.ppermute(value, "row", [(r, to(r)) for r in range(self.rows)])

    def sum_all(self, value):
        half = value.shape[0] // 2
        odd = self.col % 2 == 1
        keep = jnp.where(odd, value[half:], value[:half])
        keep = keep + self.over_col(jnp.where(odd, value[:half], value[half:]), lambda c: c ^ 1)
        for bit in self.bits()[1:]:
            keep = keep + self.over_col(keep, lambda c: c ^ bit)
        for bit in [1 << i for i in range(self.rows.bit_length() - 1)]:
            keep = keep + self.over_row(keep, lambda r: r ^ bit)
        other = self.over_col(keep, lambda c: c ^ 1)
        return jnp.concatenate([jnp.where(odd, other, keep), jnp.where(odd, keep, other)], axis=0)

    def deal(self, value):
        size = value.shape[0] // self.cols
        piece = value[:size]
        for q in range(1, self.cols):
            got = self.over_col(value[q * size : (q + 1) * size], lambda c: q if c == 0 else None)
            piece = jnp.where(self.col == q, got, piece)
        return piece

    def rows_at(self, piece, first):
        size = piece.shape[0]
        mine = (self.row * self.cols + self.col) * size
        padded = jnp.pad(piece, ((BAND, BAND), (0, 0)))
        at = jnp.clip(first - mine + BAND, 0, size + BAND)
        return lax.dynamic_slice_in_dim(padded, at, BAND, axis=0)

    def place(self, piece):
        pairs = [
            ((g * self.per + y, q), (q * self.per + y, g))
            for g in range(self.cols)
            for y in range(self.per)
            for q in range(self.cols)
        ]
        return self.over_both(piece, pairs)

    def line(self, value):
        count = self.cols
        up, down = [value], [value]
        for step in range(count - 1):
            rising = range(step, count - 1)
            for parts, move in ((up, 1), (down, -1)):
                pairs = [
                    (g * self.per + y, (g + move) * self.per + y)
                    for g in (rising if move > 0 else [count - 1 - k for k in rising])
                    for y in range(self.per)
                ]
                parts.append(lax.ppermute(parts[-1], "row", pairs))
        slots = jnp.stack(up[:0:-1] + [value] + down[1:], axis=0)
        return lax.dynamic_slice_in_dim(slots, count - 1 - self.group, count, axis=0)

    def lanes(self, value):
        value = value[None]
        bit = 1
        while bit < self.per:
            other = self.over_row(value, lambda r: r ^ bit)
            odd = (self.lane // bit) % 2 == 1
            value = jnp.concatenate([jnp.where(odd, other, value), jnp.where(odd, value, other)], axis=0)
            bit *= 2
        return value

    def line_row(self, piece):
        half = piece.shape[0] // 2
        first = jnp.swapaxes(self.line(self.lanes(piece[:half])), 0, 1)
        second = self.lanes(self.line(piece[half:]))
        return jnp.concatenate([first, second], axis=2).reshape(-1, piece.shape[1])

    def first_pieces(self, value):
        size = value.shape[0] // self.cols
        piece = None
        for q in range(self.cols):
            pairs = [
                ((g * self.per + y, 0), (q * self.per + y, g))
                for g in range(self.cols)
                for y in range(self.per)
            ]
            got = self.over_both(value[q * size : (q + 1) * size], pairs)
            piece = got if piece is None else piece + got
        return piece

    def along_row(self, piece):
        whole = lax.all_gather(piece, "row", axis=0).reshape(self.cols, self.per, -1, piece.shape[1])
        return jnp.swapaxes(whole, 0, 1).reshape(-1, piece.shape[1])


def after(value, *others):
    return lax.optimization_barrier((value, *others))[0]


def body(moves_of, matrix):
    moves = moves_of()
    m, n = matrix.shape
    size = m // moves.cols
    at = (moves.row * m + moves.col * size).astype(jnp.int32).reshape(1)
    col_at = (moves.col * n).astype(jnp.int32).reshape(1)
    one, two = BAND, 2 * BAND
    square, tall = (BAND, BAND), (2 * BAND, BAND)

    piece1 = moves.first_pieces(matrix[:, :one])
    raws = moves.deal(after(matrix[:, :two], piece1))
    raw1, raw2 = raws[:, :one], raws[:, one:two]
    raw1_c = after(moves.line_row(piece1), raws)
    gram1, high1, low1 = by_rows(gram_kernel, "gram", n, [col_at, raw1_c], [square, BF16, BF16], 2)
    gram1 = moves.total(gram1)
    heads = moves.spread(raw1_c[one : two + BAND])
    top1, low_head = heads[:BAND], heads[BAND:]
    raw2_c = moves.along_row(moves.first_pieces(after(matrix[:, one:two], high1)))
    part1 = image_of(matrix, high1, low1)
    image1 = moves.scatter_sum(part1)
    inv1 = by_steps(factor_kernel, "factor", gram1)
    y1, x1, mid1 = by_rows(first_kernel, "first", size, [at, raw1, image1, raw2, inv1], [F32, F32, square], 3)
    both = moves.sum_all(jnp.concatenate([mid1, moves.rows_at(x1, one)], axis=0))
    mid1, x1_head = both[:BAND], both[BAND:]
    tm1 = by_steps(transform_kernel, "transform", after(top1, x1), inv1)
    w1, pan2, w1_head, gram2, inner = by_rows(
        second_kernel,
        "second",
        size,
        [at, after(y1, raw2_c), x1, raw2, tm1, mid1, x1_head, top1, inv1],
        [F32, F32, square, square, tall],
        9,
    )
    placed2 = moves.place(pan2)
    pan2_c = moves.along_row(placed2)
    both = moves.sum_all(after(jnp.concatenate([gram2, moves.rows_at(pan2, two)], axis=0), placed2))
    gram2, top2 = both[:BAND], both[BAND:]
    inv2 = by_steps(factor_kernel, "factor", gram2)
    both = moves.sum_all(after(jnp.concatenate([inner, moves.rows_at(w1, two)], axis=0), gram2))
    inner, w1_next = both[: 2 * BAND], both[2 * BAND :]
    pair1 = moves.collect(after(jnp.concatenate([y1, w1], axis=1), inner))
    y1_r, w1_r = pair1[:, :BAND], pair1[:, BAND:]
    raw3 = moves.deal(after(matrix[:, two : two + BAND], placed2))
    ready = after(pan2_c, raw3, inv2)
    high2, low2 = by_rows(halves_kernel, "halves", n, [col_at, ready], [BF16, BF16], 1)
    part2 = image_of(matrix, high2, low2)
    image2 = moves.scatter_sum(part2)
    y1_c, w1_c = by_rows(
        sides_kernel, "sides", n, [col_at, raw1_c, raw2_c, after(pan2_c, part2), inv1, tm1, w1_head], [F32, F32], 3
    )
    tm2 = by_steps(transform_kernel, "transform", top2, inv2)
    x2, y2, mid2 = by_rows(
        next_kernel,
        "next",
        size,
        [at, raw3, y1, w1, w1_next, low_head, inv1, image2, after(inner, tm2), pan2, inv2],
        [F32, F32, square],
        8,
    )
    placed3 = moves.place(x2)
    x2_c = moves.along_row(placed3)
    mid2 = moves.sum_all(after(mid2, placed3))
    half = update(matrix, y1_r, after(w1_r, x2), y1_c, w1_c, "update_first", 3)
    (y2_c,) = by_rows(
        functools.partial(vectors_kernel, two), "vectors", n, [col_at, after(pan2_c, x2), inv2], [F32], 1
    )
    (w2,) = by_rows(last_kernel, "last", size, [y2, x2, tm2, mid2], [F32], 2)
    pair2 = moves.collect(jnp.concatenate([y2, w2], axis=1))
    y2_r, w2_r = pair2[:, :BAND], pair2[:, BAND:]
    (w2_c,) = by_rows(last_kernel, "last", n, [y2_c, x2_c, tm2, mid2], [F32], 2)
    updated = update(half, y2_r, w2_r, y2_c, w2_c, "update_second")
    return updated, jnp.concatenate([y1_r, y2_r], axis=1)


def solution(mesh):
    def run(matrix):
        return body(lambda: Moves(mesh), matrix)

    return jax.shard_map(
        run,
        mesh=mesh,
        in_specs=(P("row", "col"),),
        out_specs=(P("row", "col"), P("row", None)),
        check_vma=False,
    )
```

time: 1710 us -> 798 us (0.47)
  waiting for transfers between devices: 928 us -> 181 us
  matrix products: 460 us -> 0 us
  Pallas kernels: 0 us -> 342 us
  other arithmetic: 258 us -> 43.3 us
  starting transfers between devices: 0.8 us -> 161 us
    psum x8 -> x0, waiting for transfers between devices: 928 us -> none  [the longest x4 729 us: body(): lax.psum((contract_first(panel_rows, panel_rows), contract_first(unit_row...]
    dot_general x32 -> x0, matrix products: 430 us -> none  [the longest x8 203 us: contract_first(): lax.dot_general(left, right, (((0,), (0,)), ((), ())), precision=lax.Prec...]
    pallas_call x0 -> x31, Pallas kernels: none -> 342 us  [the longest x16 130 us: by_steps(): pl.pallas_call(functools.partial(kernel, at), out_shape=jax.ShapeDtypeStr...]
    another operation x36 -> x8, other arithmetic: 218 us -> 7.87 us  [collect(): jnp.stack([jnp.where(odd, other, piece), jnp.where(odd, piece, other)], a...]
    ppermute x0 -> x66, waiting for transfers between devices: none -> 181 us  [the longest x14 71.7 us: over_row(): return lax.ppermute(value, 'row', [(r, to(r)) for r in range(self.rows)])]
    ppermute x0 -> x66, starting transfers between devices: none -> 161 us  [the longest x30 90.7 us: over_col(): lax.ppermute(value, 'col', [(c, to(c)) for c in range(self.cols) if to(c)...]
    another operation x32 -> x0, matrix products: 30.8 us -> none  [the longest x6 13 us: body(): jax.scipy.linalg.solve_triangular(factor_low, row_strip, lower=True)]
    slice x0 -> x12, local copies, waits for them, and re-layouts: none -> 23.5 us  [the longest x1 5.03 us: body(): raws = moves.deal(after(matrix[:, :two], piece1))]
  transfers between devices with their start and end apart: 8 -> 69, of which waited for: 8 -> 33; matrix products, arithmetic and copies ran while one was open for 3% -> 9% of each run, Pallas kernels for 0% -> 35%
where the time goes in v1:
time: 798 us; the launch traced here: 789 us
  Pallas kernels  342 us (43%)
  waiting for transfers between devices  181 us (23%)
  starting transfers between devices  161 us (20%)
  local copies, waits for them, and re-layouts  46.1 us (6%)
  other arithmetic  43.3 us (5%)
  between operations  15.1 us (2%)
    pallas_call x16, Pallas kernels, by_steps(): pl.pallas_call(functools.partial(kernel, at), out_shape=jax.ShapeDtypeStr...  130 us
    pallas_call x4, Pallas kernels, update(): pl.pallas_call(update_kernel, grid=(each,), in_specs=specs, out_specs=pl....  102 us
    ppermute x30, starting transfers between devices, over_col(): lax.ppermute(value, 'col', [(c, to(c)) for c in range(self.cols) if to(c)...  90.7 us
    ppermute x14, waiting for transfers between devices, over_row(): return lax.ppermute(value, 'row', [(r, to(r)) for r in range(self.rows)])  71.7 us
    pallas_call x9, Pallas kernels, by_rows(): pl.pallas_call(kernel, grid=(rows // tile,), in_specs=in_specs, out_specs...  62.3 us
    pallas_call x2, Pallas kernels, image_of(): pl.pallas_call(image_kernel, grid=(n // deep,), in_specs=[pl.BlockSpec((m...  48.6 us
    ppermute x30, waiting for transfers between devices, over_col(): lax.ppermute(value, 'col', [(c, to(c)) for c in range(self.cols) if to(c)...  46.4 us
    ppermute x12, waiting for transfers between devices, line(): parts.append(lax.ppermute(parts[-1], 'row', pairs))  40.4 us
  transfers between devices with their start and end apart: 69, of which 33 were waited for; matrix products, arithmetic and copies ran while one was open for 9% of the time, Pallas kernels for 35%

profile of v1, /device:TPU:0, one launch (start us, length us, event | category | flops | bytes accessed | tf_op | source)
XLA Modules:
  0.0 788.6 jit_solution(12293795741728964727)
XLA Ops:
  36.3 8.2 %collective-permute-start.14 = (f32[288,256]{1,0:T(8,128)S(1)}, f32[288,256]{1,0:T(8,128)S(1)}, u32[]{:S(2)}, u32[]{:S(2)}) collective-permute-start(f32[288,256]{1,0:T(8,128)S(1)} %get-tuple-element.106), channel_id=1, source_target_pairs={{0,8},{4,12},{8,16},{12,20},{16,24},{20,28},{1,9},{5,13},{9,17},{1... | collective-permute-start | bytes 884744 | tf_op jit(solution)/shard_map/ppermute | solution.py:479
  106.8 15.1 %collective-permute-done.12 = f32[2,288,256]{2,1,0:T(8,128)S(1)} collective-permute-done((f32[2,288,256]{2,1,0:T(8,128)S(1)}, f32[2,288,256]{2,1,0:T(8,128)S(1)}, u32[]{:S(2)}, u32[]{:S(2)}) %collective-permute-start.12) | collective-permute-done | bytes 589856 | tf_op jit(solution)/shard_map/ppermute | solution.py:479
  123.4 10.2 %collective-permute-done.13 = f32[2,288,256]{2,1,0:T(8,128)S(1)} collective-permute-done((f32[2,288,256]{2,1,0:T(8,128)S(1)}, f32[2,288,256]{2,1,0:T(8,128)S(1)}, u32[]{:S(2)}, u32[]{:S(2)}) %collective-permute-start.13) | collective-permute-done | bytes 589856 | tf_op jit(solution)/shard_map/ppermute | solution.py:479
  137.0 8.5 %gram.1 = (f32[256,256]{1,0:T(8,128)}, bf16[4608,256]{1,0:T(8,128)(2,1)}, bf16[4608,256]{1,0:T(8,128)(2,1)}) custom-call(s32[1]{0:T(128)} %bitcast.1.offset_ref, f32[4608,256]{1,0:T(8,128)} %bitcast.121), custom_call_target="tpu_custom_call" | custom-call | flops 7247757312 | bytes 28311552 | tf_op jit(solution)/shard_map/gram/pallas_call | solution.py:266
  169.8 24.4 %image.2 = f32[2304,256]{1,0:T(8,128)} custom-call(f32[2304,4608]{1,0:T(8,128)} %matrix_ref.9, bf16[4608,256]{1,0:T(8,128)(2,1)} %get-tuple-element.37.high_ref, bf16[4608,256]{1,0:T(8,128)(2,1)} %get-tuple-element.38.low_ref), custom_call_target="tpu_custom_call" | custom-call | flops 21743271936 | bytes 42467328 | tf_op jit(solution)/shard_map/image/pallas_call | solution.py:305
  205.7 8.1 %factor.8.start_ref = f32[256,512]{1,0:T(8,128)} custom-call(f32[256,256]{1,0:T(8,128)} %add.171.start_ref), custom_call_target="tpu_custom_call" | custom-call | flops 6000000000 | bytes 4000000 | tf_op jit(solution)/shard_map/factor/pallas_call | solution.py:117
  213.8 8.2 %factor.9.start_ref = f32[256,512]{1,0:T(8,128)} custom-call(f32[256,512]{1,0:T(8,128)} %factor.8.start_ref), custom_call_target="tpu_custom_call" | custom-call | flops 6000000000 | bytes 4000000 | tf_op jit(solution)/shard_map/factor/pallas_call | solution.py:117
  225.1 8.1 %factor.10.start_ref = f32[256,512]{1,0:T(8,128)} custom-call(f32[256,512]{1,0:T(8,128)} %factor.9.start_ref), custom_call_target="tpu_custom_call" | custom-call | flops 6000000000 | bytes 4000000 | tf_op jit(solution)/shard_map/factor/pallas_call | solution.py:117
  261.0 8.5 %transform.8.refs_0_ = f32[256,512]{1,0:T(8,128)} custom-call(f32[256,256]{1,0:T(8,128)} %get-tuple-element.44.refs_0_.top_ref, f32[256,256]{1,0:T(8,128)} %factor.11.inv_ref.refs_1_), custom_call_target="tpu_custom_call" | custom-call | flops 6000000000 | bytes 4000000 | tf_op jit(solution)/shard_map/transform/pallas_call | solution.py:117
  276.4 8.1 %transform.9.refs_0_ = f32[256,512]{1,0:T(8,128)} custom-call(f32[256,512]{1,0:T(8,128)} %transform.8.refs_0_), custom_call_target="tpu_custom_call" | custom-call | flops 6000000000 | bytes 4000000 | tf_op jit(solution)/shard_map/transform/pallas_call | solution.py:117
  284.7 8.2 %transform.10.refs_0_ = f32[256,512]{1,0:T(8,128)} custom-call(f32[256,512]{1,0:T(8,128)} %transform.9.refs_0_), custom_call_target="tpu_custom_call" | custom-call | flops 6000000000 | bytes 4000000 | tf_op jit(solution)/shard_map/transform/pallas_call | solution.py:117
  321.9 18.5 %collective-permute-start.38 = (f32[256,256]{1,0:T(8,128)S(1)}, f32[256,256]{1,0:T(8,128)S(1)}, u32[]{:S(2)}, u32[]{:S(2)}) collective-permute-start(f32[256,256]{1,0:T(8,128)S(1)} %slice_select_fusion.1), channel_id=1, source_target_pairs={{0,1},{1,0},{2,3},{3,2},{4,5},{5,4},{6,7},{7,6},{8,9},{9,8},{10,11... | collective-permute-start | bytes 786440 | tf_op jit(solution)/shard_map/ppermute | solution.py:386
  341.6 9.9 %collective-permute-start.39 = (f32[256,256]{1,0:T(8,128)S(1)}, f32[256,256]{1,0:T(8,128)S(1)}, u32[]{:S(2)}, u32[]{:S(2)}) collective-permute-start(f32[256,256]{1,0:T(8,128)S(1)} %select_add_fusion.1), channel_id=1, source_target_pairs={{0,2},{1,3},{2,0},{3,1},{4,6},{5,7},{6,4},{7,5},{8,10},{9,11},{10,... | collective-permute-start | bytes 786440 | tf_op jit(solution)/shard_map/ppermute | solution.py:386
  358.5 10.2 %collective-permute-done.40 = f32[256,256]{1,0:T(8,128)S(1)} collective-permute-done((f32[256,256]{1,0:T(8,128)S(1)}, f32[256,256]{1,0:T(8,128)S(1)}, u32[]{:S(2)}, u32[]{:S(2)}) %collective-permute-start.40) | collective-permute-done | bytes 262176 | tf_op jit(solution)/shard_map/ppermute | solution.py:430
  370.2 11.9 %collective-permute-done.41 = f32[256,256]{1,0:T(8,128)S(1)} collective-permute-done((f32[256,256]{1,0:T(8,128)S(1)}, f32[256,256]{1,0:T(8,128)S(1)}, u32[]{:S(2)}, u32[]{:S(2)}) %collective-permute-start.41) | collective-permute-done | bytes 262176 | tf_op jit(solution)/shard_map/ppermute | solution.py:430
  384.1 29.0 %collective-permute-done.42 = f32[256,256]{1,0:T(8,128)S(1)} collective-permute-done((f32[256,256]{1,0:T(8,128)S(1)}, f32[256,256]{1,0:T(8,128)S(1)}, u32[]{:S(2)}, u32[]{:S(2)}) %collective-permute-start.42) | collective-permute-done | bytes 262176 | tf_op jit(solution)/shard_map/ppermute | solution.py:430
  422.9 8.2 %collective-permute-done.52 = f32[576,256]{1,0:T(8,128)S(1)} collective-permute-done((f32[576,256]{1,0:T(8,128)S(1)}, f32[576,256]{1,0:T(8,128)S(1)}, u32[]{:S(2)}, u32[]{:S(2)}) %collective-permute-start.52) | collective-permute-done | bytes 589856 | tf_op jit(solution)/shard_map/ppermute | solution.py:386
  443.1 8.2 %factor.12.start_ref = f32[256,512]{1,0:T(8,128)} custom-call(f32[256,256]{1,0:T(8,128)} %get-tuple-element.108.start_ref), custom_call_target="tpu_custom_call" | custom-call | flops 6000000000 | bytes 4000000 | tf_op jit(solution)/shard_map/factor/pallas_call | solution.py:117
  451.4 8.1 %factor.13.start_ref = f32[256,512]{1,0:T(8,128)} custom-call(f32[256,512]{1,0:T(8,128)} %factor.12.start_ref), custom_call_target="tpu_custom_call" | custom-call | flops 6000000000 | bytes 4000000 | tf_op jit(solution)/shard_map/factor/pallas_call | solution.py:117
  462.7 8.1 %factor.14.start_ref = f32[256,512]{1,0:T(8,128)} custom-call(f32[256,512]{1,0:T(8,128)} %factor.13.start_ref), custom_call_target="tpu_custom_call" | custom-call | flops 6000000000 | bytes 4000000 | tf_op jit(solution)/shard_map/factor/pallas_call | solution.py:117
  497.1 24.2 %image.3 = f32[2304,256]{1,0:T(8,128)} custom-call(f32[2304,4608]{1,0:T(8,128)} %matrix_ref.9, bf16[4608,256]{1,0:T(8,128)(2,1)} %get-tuple-element.55.high_ref, bf16[4608,256]{1,0:T(8,128)(2,1)} %get-tuple-element.56.low_ref), custom_call_target="tpu_custom_call" | custom-call | flops 21743271936 | bytes 42467328 | tf_op jit(solution)/shard_map/image/pallas_call | solution.py:305
  524.3 8.5 %transform.12.refs_0_ = f32[256,512]{1,0:T(8,128)} custom-call(f32[256,256]{1,0:T(8,128)} %get-tuple-element.107.refs_0_, f32[256,256]{1,0:T(8,128)} %factor.15.refs_1_.new_ref.inv_ref), custom_call_target="tpu_custom_call" | custom-call | flops 6000000000 | bytes 4000000 | tf_op jit(solution)/shard_map/transform/pallas_call | solution.py:117
  532.8 8.1 %transform.13.refs_0_ = f32[256,512]{1,0:T(8,128)} custom-call(f32[256,512]{1,0:T(8,128)} %transform.12.refs_0_), custom_call_target="tpu_custom_call" | custom-call | flops 6000000000 | bytes 4000000 | tf_op jit(solution)/shard_map/transform/pallas_call | solution.py:117
  547.7 8.1 %transform.14.refs_0_ = f32[256,512]{1,0:T(8,128)} custom-call(f32[256,512]{1,0:T(8,128)} %transform.13.refs_0_), custom_call_target="tpu_custom_call" | custom-call | flops 6000000000 | bytes 4000000 | tf_op jit(solution)/shard_map/transform/pallas_call | solution.py:117
  576.2 12.8 %collective-permute-start.58 = (f32[128,256]{1,0:T(8,128)S(1)}, f32[128,256]{1,0:T(8,128)S(1)}, u32[]{:S(2)}, u32[]{:S(2)}) collective-permute-start(f32[128,256]{1,0:T(8,128)S(1)} %slice_select_fusion.2), channel_id=1, source_target_pairs={{0,1},{1,0},{2,3},{3,2},{4,5},{5,4},{6,7},{7,6},{8,9},{9,8},{10,11... | collective-permute-start | bytes 393224 | tf_op jit(solution)/shard_map/ppermute | solution.py:386
  591.0 17.8 %collective-permute-start.59 = (f32[128,256]{1,0:T(8,128)S(1)}, f32[128,256]{1,0:T(8,128)S(1)}, u32[]{:S(2)}, u32[]{:S(2)}) collective-permute-start(f32[128,256]{1,0:T(8,128)S(1)} %select_add_fusion.3), channel_id=1, source_target_pairs={{0,2},{1,3},{2,0},{3,1},{4,6},{5,7},{6,4},{7,5},{8,10},{9,11},{10,... | collective-permute-start | bytes 393224 | tf_op jit(solution)/shard_map/ppermute | solution.py:386
  622.9 13.7 %sides.1 = (f32[4608,256]{1,0:T(8,128)}, f32[4608,256]{1,0:T(8,128)}) custom-call(s32[1]{0:T(128)} %bitcast.1.offset_ref, f32[4608,256]{1,0:T(8,128)} %bitcast.124, f32[4608,256]{1,0:T(8,128)} %bitcast.125, f32[4608,256]{1,0:T(8,128)} %bitcast.128, f32[256,256]{1,0:T(8,128)} %factor.11.inv_ref.refs_1_, f32[256,256]{1,0:T(8,128)} %transform.11.tm_ref, ...), custom_call_target="tpu_custom_call" | custom-call | flops 10871635968 | bytes 28311552 | tf_op jit(solution)/shard_map/sides/pallas_call | solution.py:266
  650.0 19.3 %update_first.3.rest_0_ = f32[2304,4608]{1,0:T(8,128)} custom-call(f32[2304,4608]{1,0:T(8,128)} %matrix_ref.9, f32[2304,256]{1,0:T(8,128)} %get-tuple-element.79.yr_ref, f32[2304,256]{1,0:T(8,128)} %get-tuple-element.59.wr_ref, f32[4608,256]{1,0:T(8,128)} %get-tuple-element.62.yc_ref, f32[4608,256]{1,0:T(8,128)} %get-tuple-element.63.wc_ref), custom_call_target="tpu_custom_call" | custom-call | flops 14495514624 | bytes 28311552 | tf_op jit(solution)/shard_map/update_first/pallas_call | solution.py:358
  677.4 19.3 %update_first.4.rest_0_ = f32[2304,4608]{1,0:T(8,128)} custom-call(f32[2304,4608]{1,0:T(8,128)} %matrix_ref.9, f32[2304,256]{1,0:T(8,128)} %get-tuple-element.79.yr_ref, f32[2304,256]{1,0:T(8,128)} %get-tuple-element.59.wr_ref, f32[4608,256]{1,0:T(8,128)} %get-tuple-element.62.yc_ref, ...), custom_call_target="tpu_custom_call", output_to_operand_aliasing={{}: (5, {})} | custom-call | flops 14495514624 | bytes 28311552 | tf_op jit(solution)/shard_map/update_first/pallas_call | solution.py:358
  696.7 19.4 %update_first.5.matrix_ref = f32[2304,4608]{1,0:T(8,128)} custom-call(f32[2304,4608]{1,0:T(8,128)} %matrix_ref.9, f32[2304,256]{1,0:T(8,128)} %get-tuple-element.79.yr_ref, f32[2304,256]{1,0:T(8,128)} %get-tuple-element.59.wr_ref, f32[4608,256]{1,0:T(8,128)} %get-tuple-element.62.yc_ref, ...), custom_call_target="tpu_custom_call", output_to_operand_aliasing={{}: (5, {})} | custom-call | flops 14495514624 | bytes 28311552 | tf_op jit(solution)/shard_map/update_first/pallas_call | solution.py:358
  728.1 9.9 %last.3.wc_ref = f32[4608,256]{1,0:T(8,128)} custom-call(f32[4608,256]{1,0:T(8,128)} %vectors.1.y_ref.yc_ref, f32[4608,256]{1,0:T(8,128)} %bitcast.132, f32[256,256]{1,0:T(8,128)} %transform.15.tm_ref, f32[256,256]{1,0:T(8,128)} %pad_maximum_fusion.11.mid_ref), custom_call_target="tpu_custom_call" | custom-call | flops 7247757312 | bytes 28311552 | tf_op jit(solution)/shard_map/last/pallas_call | solution.py:266
  738.0 43.7 %update_second.1 = f32[2304,4608]{1,0:T(8,128)} custom-call(f32[2304,4608]{1,0:T(8,128)} %update_first.5.matrix_ref, f32[2304,256]{1,0:T(8,128)} %copy-done.4, f32[2304,256]{1,0:T(8,128)} %get-tuple-element.74.wr_ref, f32[4608,256]{1,0:T(8,128)} %vectors.1.y_ref.yc_ref, f32[4608,256]{1,0:T(8,128)} %last.3.wc_ref), custom_call_target="tpu_custom_call" | custom-call | flops 43486543872 | bytes 84934656 | tf_op jit(solution)/shard_map/update_second/pallas_call | solution.py:358
  (267 shorter events, 341.2 us)
Async XLA Ops:
  7.2 299.4 %all-gather.7.cloned.1.call-start = ((), (), s32[]{:S(2)}) async-start(), calls=%async_computation | async-start | bytes 5308416 | tf_op jit(solution)/shard_map/all_gather | solution.py:513
  20.1 15.9 %collective-permute-start.1 = (f32[576,256]{1,0:T(8,128)S(1)}, f32[576,256]{1,0:T(8,128)S(1)}, u32[]{:S(2)}, u32[]{:S(2)}) collective-permute-start(f32[576,256]{1,0:T(8,128)S(1)} %get-tuple-element.70), channel_id=1, source_target_pairs={{0,8},{4,12},{8,9},{12,13},{16,10},{20,14},{24,11},{28,15}} | collective-permute-start | bytes 1769480 | tf_op jit(solution)/shard_map/ppermute | solution.py:390
  57.7 15.0 %collective-permute-start.16 = (f32[288,256]{1,0:T(8,128)S(1)}, f32[288,256]{1,0:T(8,128)S(1)}, u32[]{:S(2)}, u32[]{:S(2)}) collective-permute-start(f32[288,256]{1,0:T(8,128)S(1)} %collective-permute-done.15), channel_id=1, source_target_pairs={{16,24},{20,28},{17,25},{21,29},{18,26},{22,30},{19,27},{23,31}} | collective-permute-start | bytes 884744 | tf_op jit(solution)/shard_map/ppermute | solution.py:479
  60.7 26.8 %collective-permute-start.4 = (f32[576,512]{1,0:T(8,128)S(1)}, f32[576,512]{1,0:T(8,128)S(1)}, u32[]{:S(2)}, u32[]{:S(2)}) collective-permute-start(f32[576,512]{1,0:T(8,128)S(1)} %get-tuple-element.84), channel_id=1, source_target_pairs={{0,3},{4,7},{8,11},{12,15},{16,19},{20,23},{24,27},{28,31}} | collective-permute-start | bytes 3538952 | tf_op jit(solution)/shard_map/ppermute | solution.py:386
  62.1 42.5 %collective-permute-start.5 = (f32[576,512]{1,0:T(8,128)S(1)}, f32[576,512]{1,0:T(8,128)S(1)}, u32[]{:S(2)}, u32[]{:S(2)}) collective-permute-start(f32[576,512]{1,0:T(8,128)S(1)} %get-tuple-element.83), channel_id=1, source_target_pairs={{0,2},{4,6},{8,10},{12,14},{16,18},{20,22},{24,26},{28,30}} | collective-permute-start | bytes 3538952 | tf_op jit(solution)/shard_map/ppermute | solution.py:386
  69.7 34.9 %collective-permute-start.6 = (f32[576,512]{1,0:T(8,128)S(1)}, f32[576,512]{1,0:T(8,128)S(1)}, u32[]{:S(2)}, u32[]{:S(2)}) collective-permute-start(f32[576,512]{1,0:T(8,128)S(1)} %get-tuple-element.82), channel_id=1, source_target_pairs={{0,1},{4,5},{8,9},{12,13},{16,17},{20,21},{24,25},{28,29}} | collective-permute-start | bytes 3538952 | tf_op jit(solution)/shard_map/ppermute | solution.py:386
  86.1 16.5 %collective-permute-start.11 = (f32[2,288,256]{2,1,0:T(8,128)S(1)}, f32[2,288,256]{2,1,0:T(8,128)S(1)}, u32[]{:S(2)}, u32[]{:S(2)}) collective-permute-start(f32[2,288,256]{2,1,0:T(8,128)S(1)} %pad_maximum_fusion.8), channel_id=1, source_target_pairs={{24,16},{28,20},{16,8},{20,12},{8,0},{12,4},{25,17},{29,21},{17,9}... | collective-permute-start | bytes 1769480 | tf_op jit(solution)/shard_map/ppermute | solution.py:479
  87.5 18.9 %collective-permute-start.20 = (f32[1,4,288,256]{3,2,0,1:T(8,128)S(1)}, f32[1,4,288,256]{3,2,0,1:T(8,128)S(1)}, u32[]{:S(2)}, u32[]{:S(2)}) collective-permute-start(f32[1,4,288,256]{3,2,0,1:T(8,128)S(1)} %dynamic-slice_bitcast_fusion.1), channel_id=1, source_target_pairs={{0,4},{4,0},{8,12},{12,8},{16,20},{20,16},{24,28},{28,24},{1,5},{5... | collective-permute-start | bytes 3538952 | tf_op jit(solution)/shard_map/ppermute | solution.py:430
  102.6 19.2 %collective-permute-start.12 = (f32[2,288,256]{2,1,0:T(8,128)S(1)}, f32[2,288,256]{2,1,0:T(8,128)S(1)}, u32[]{:S(2)}, u32[]{:S(2)}) collective-permute-start(f32[2,288,256]{2,1,0:T(8,128)S(1)} %collective-permute-done.11), channel_id=1, source_target_pairs={{16,8},{20,12},{8,0},{12,4},{17,9},{21,13},{9,1},{13,5},{18,10},{2... | collective-permute-start | bytes 1769480 | tf_op jit(solution)/shard_map/ppermute | solution.py:479
  103.9 19.2 %collective-permute-start.10 = (f32[2,288,256]{2,1,0:T(8,128)S(1)}, f32[2,288,256]{2,1,0:T(8,128)S(1)}, u32[]{:S(2)}, u32[]{:S(2)}) collective-permute-start(f32[2,288,256]{2,1,0:T(8,128)S(1)} %collective-permute-done.9), channel_id=1, source_target_pairs={{16,24},{20,28},{17,25},{21,29},{18,26},{22,30},{19,27},{23,31}} | collective-permute-start | bytes 1769480 | tf_op jit(solution)/shard_map/ppermute | solution.py:479
  151.4 15.6 %collective-permute-start.26 = (f32[576,256]{1,0:T(8,128)S(1)}, f32[576,256]{1,0:T(8,128)}, u32[]{:S(2)}, u32[]{:S(2)}) collective-permute-start(f32[576,256]{1,0:T(8,128)S(1)} %get-tuple-element.92), channel_id=1, source_target_pairs={{0,8},{4,12},{8,9},{12,13},{16,10},{20,14},{24,11},{28,15}} | collective-permute-start | bytes 1769480 | tf_op jit(solution)/shard_map/ppermute | solution.py:390
  157.3 40.7 %collective-permute-start.29 = (f32[512,256]{1,0:T(8,128)}, f32[512,256]{1,0:T(8,128)}, u32[]{:S(2)}, u32[]{:S(2)}) collective-permute-start(f32[512,256]{1,0:T(8,128)} %slice.171), channel_id=1, source_target_pairs={{0,2},{4,6},{8,10},{12,14},{16,18},{20,22},{24,26},{28,30}} | collective-permute-start | bytes 1572872 | tf_op jit(solution)/shard_map/ppermute | solution.py:386
  169.6 317.5 %all-gather.9.cloned.1.call-start = ((), (), s32[]{:S(2)}) async-start(), calls=%async_computation.1 | async-start | bytes 5308416 | tf_op jit(solution)/shard_map/all_gather | solution.py:513
  196.0 26.1 %collective-permute-start.21 = (f32[2,576,256]{2,1,0:T(8,128)S(1)}, f32[2,576,256]{2,1,0:T(8,128)}, u32[]{:S(2)}, u32[]{:S(2)}) collective-permute-start(f32[2,576,256]{2,1,0:T(8,128)S(1)} %select_bitcast_fusion.9), channel_id=1, source_target_pairs={{0,1},{1,0},{2,3},{3,2},{4,5},{5,4},{6,7},{7,6},{8,9},{9,8},{10,11... | collective-permute-start | bytes 3538952 | tf_op jit(solution)/shard_map/ppermute | solution.py:386
  200.0 49.7 %collective-permute-start.30 = (f32[512,256]{1,0:T(8,128)}, f32[512,256]{1,0:T(8,128)}, u32[]{:S(2)}, u32[]{:S(2)}) collective-permute-start(f32[512,256]{1,0:T(8,128)} %broadcast_select_fusion.2), channel_id=1, source_target_pairs={{0,1},{2,3},{4,5},{6,7},{8,9},{10,11},{12,13},{14,15},{16,17},{18,... | collective-permute-start | bytes 1572872 | tf_op jit(solution)/shard_map/ppermute | solution.py:386
  223.7 17.1 %collective-permute-start.22 = (f32[576,256]{1,0:T(8,128)S(1)}, f32[576,256]{1,0:T(8,128)S(1)}, u32[]{:S(2)}, u32[]{:S(2)}) collective-permute-start(f32[576,256]{1,0:T(8,128)S(1)} %select_bitcast_fusion.11), channel_id=1, source_target_pairs={{0,2},{1,3},{2,0},{3,1},{4,6},{5,7},{6,4},{7,5},{8,10},{9,11},{10,... | collective-permute-start | bytes 1769480 | tf_op jit(solution)/shard_map/ppermute | solution.py:386
  269.5 15.0 %collective-permute-start.34 = (f32[256,256]{1,0:T(8,128)S(1)}, f32[256,256]{1,0:T(8,128)S(1)}, u32[]{:S(2)}, u32[]{:S(2)}) collective-permute-start(f32[256,256]{1,0:T(8,128)S(1)} %add.180), channel_id=1, source_target_pairs={{0,8},{4,12},{8,0},{12,4},{16,24},{20,28},{24,16},{28,20},{1,9},{5... | collective-permute-start | bytes 786440 | tf_op jit(solution)/shard_map/ppermute | solution.py:430
  319.8 403.4 %all-gather.11.cloned.1.call-start = ((), (), s32[]{:S(2)}) async-start(), calls=%async_computation.2 | async-start | bytes 5308416 | tf_op jit(solution)/shard_map/all_gather | solution.py:513
  321.9 19.7 %collective-permute-start.38 = (f32[256,256]{1,0:T(8,128)S(1)}, f32[256,256]{1,0:T(8,128)S(1)}, u32[]{:S(2)}, u32[]{:S(2)}) collective-permute-start(f32[256,256]{1,0:T(8,128)S(1)} %slice_select_fusion.1), channel_id=1, source_target_pairs={{0,1},{1,0},{2,3},{3,2},{4,5},{5,4},{6,7},{7,6},{8,9},{9,8},{10,11... | collective-permute-start | bytes 786440 | tf_op jit(solution)/shard_map/ppermute | solution.py:386
  341.6 16.5 %collective-permute-start.39 = (f32[256,256]{1,0:T(8,128)S(1)}, f32[256,256]{1,0:T(8,128)S(1)}, u32[]{:S(2)}, u32[]{:S(2)}) collective-permute-start(f32[256,256]{1,0:T(8,128)S(1)} %select_add_fusion.1), channel_id=1, source_target_pairs={{0,2},{1,3},{2,0},{3,1},{4,6},{5,7},{6,4},{7,5},{8,10},{9,11},{10,... | collective-permute-start | bytes 786440 | tf_op jit(solution)/shard_map/ppermute | solution.py:386
  382.1 31.0 %collective-permute-start.42 = (f32[256,256]{1,0:T(8,128)S(1)}, f32[256,256]{1,0:T(8,128)S(1)}, u32[]{:S(2)}, u32[]{:S(2)}) collective-permute-start(f32[256,256]{1,0:T(8,128)S(1)} %add.187), channel_id=1, source_target_pairs={{0,16},{4,20},{8,24},{12,28},{16,0},{20,4},{24,8},{28,12},{1,17},{... | collective-permute-start | bytes 786440 | tf_op jit(solution)/shard_map/ppermute | solution.py:430
  416.0 15.1 %collective-permute-start.52 = (f32[576,256]{1,0:T(8,128)S(1)}, f32[576,256]{1,0:T(8,128)S(1)}, u32[]{:S(2)}, u32[]{:S(2)}) collective-permute-start(f32[576,256]{1,0:T(8,128)S(1)} %get-tuple-element.89), channel_id=1, source_target_pairs={{0,3},{4,7},{8,11},{12,15},{16,19},{20,23},{24,27},{28,31}} | collective-permute-start | bytes 1769480 | tf_op jit(solution)/shard_map/ppermute | solution.py:386
  419.5 17.9 %collective-permute-start.53 = (f32[576,256]{1,0:T(8,128)S(1)}, f32[576,256]{1,0:T(8,128)S(1)}, u32[]{:S(2)}, u32[]{:S(2)}) collective-permute-start(f32[576,256]{1,0:T(8,128)S(1)} %get-tuple-element.88), channel_id=1, source_target_pairs={{0,2},{4,6},{8,10},{12,14},{16,18},{20,22},{24,26},{28,30}} | collective-permute-start | bytes 1769480 | tf_op jit(solution)/shard_map/ppermute | solution.py:386
  420.8 16.5 %collective-permute-start.54 = (f32[576,256]{1,0:T(8,128)S(1)}, f32[576,256]{1,0:T(8,128)S(1)}, u32[]{:S(2)}, u32[]{:S(2)}) collective-permute-start(f32[576,256]{1,0:T(8,128)S(1)} %get-tuple-element.87), channel_id=1, source_target_pairs={{0,1},{4,5},{8,9},{12,13},{16,17},{20,21},{24,25},{28,29}} | collective-permute-start | bytes 1769480 | tf_op jit(solution)/shard_map/ppermute | solution.py:386
  422.6 18.9 %collective-permute-start.45 = (f32[384,256]{1,0:T(8,128)S(1)}, f32[384,256]{1,0:T(8,128)S(1)}, u32[]{:S(2)}, u32[]{:S(2)}) collective-permute-start(f32[384,256]{1,0:T(8,128)S(1)} %select_add_fusion), channel_id=1, source_target_pairs={{0,2},{1,3},{2,0},{3,1},{4,6},{5,7},{6,4},{7,5},{8,10},{9,11},{10,... | collective-permute-start | bytes 1179656 | tf_op jit(solution)/shard_map/ppermute | solution.py:386
  483.8 57.2 %collective-permute-start.50 = (f32[576,512]{1,0:T(8,128)S(1)}, f32[576,512]{1,0:T(8,128)}, u32[]{:S(2)}, u32[]{:S(2)}) collective-permute-start(f32[576,512]{1,0:T(8,128)S(1)} %pad_maximum_fusion.5), channel_id=1, source_target_pairs={{0,2},{1,3},{2,0},{3,1},{4,6},{5,7},{6,4},{7,5},{8,10},{9,11},{10,... | collective-permute-start | bytes 3538952 | tf_op jit(solution)/shard_map/ppermute | solution.py:386
  524.1 20.4 %collective-permute-start.55 = (f32[2,576,256]{2,1,0:T(8,128)}, f32[2,576,256]{2,1,0:T(8,128)}, u32[]{:S(2)}, u32[]{:S(2)}) collective-permute-start(f32[2,576,256]{2,1,0:T(8,128)} %select_bitcast_fusion.6), channel_id=1, source_target_pairs={{0,1},{1,0},{2,3},{3,2},{4,5},{5,4},{6,7},{7,6},{8,9},{9,8},{10,11... | collective-permute-start | bytes 3538952 | tf_op jit(solution)/shard_map/ppermute | solution.py:386
  544.2 64.6 %collective-permute-start.51 = (f32[2,576,512]{2,1,0:T(8,128)}, f32[2,576,512]{2,1,0:T(8,128)}, u32[]{:S(2)}, u32[]{:S(2)}) collective-permute-start(f32[2,576,512]{2,1,0:T(8,128)} %pad_maximum_fusion.3), channel_id=1, source_target_pairs={{0,1},{1,0},{2,3},{3,2},{4,5},{5,4},{6,7},{7,6},{8,9},{9,8},{10,11... | collective-permute-start | bytes 7077896 | tf_op jit(solution)/shard_map/ppermute | solution.py:386
  547.4 18.0 %collective-permute-start.56 = (f32[576,256]{1,0:T(8,128)}, f32[576,256]{1,0:T(8,128)}, u32[]{:S(2)}, u32[]{:S(2)}) collective-permute-start(f32[576,256]{1,0:T(8,128)} %select_bitcast_fusion.10), channel_id=1, source_target_pairs={{0,2},{1,3},{2,0},{3,1},{4,6},{5,7},{6,4},{7,5},{8,10},{9,11},{10,... | collective-permute-start | bytes 1769480 | tf_op jit(solution)/shard_map/ppermute | solution.py:386
  591.0 21.6 %collective-permute-start.59 = (f32[128,256]{1,0:T(8,128)S(1)}, f32[128,256]{1,0:T(8,128)S(1)}, u32[]{:S(2)}, u32[]{:S(2)}) collective-permute-start(f32[128,256]{1,0:T(8,128)S(1)} %select_add_fusion.3), channel_id=1, source_target_pairs={{0,2},{1,3},{2,0},{3,1},{4,6},{5,7},{6,4},{7,5},{8,10},{9,11},{10,... | collective-permute-start | bytes 393224 | tf_op jit(solution)/shard_map/ppermute | solution.py:386
  648.3 28.4 %collective-permute-start.64 = (f32[576,512]{1,0:T(8,128)S(1)}, f32[576,512]{1,0:T(8,128)S(1)}, u32[]{:S(2)}, u32[]{:S(2)}) collective-permute-start(f32[576,512]{1,0:T(8,128)S(1)} %pad_maximum_fusion.6), channel_id=1, source_target_pairs={{0,2},{1,3},{2,0},{3,1},{4,6},{5,7},{6,4},{7,5},{8,10},{9,11},{10,... | collective-permute-start | bytes 3538952 | tf_op jit(solution)/shard_map/ppermute | solution.py:386
  677.3 38.9 %collective-permute-start.65 = (f32[2,576,512]{2,1,0:T(8,128)S(1)}, f32[2,576,512]{2,1,0:T(8,128)S(1)}, u32[]{:S(2)}, u32[]{:S(2)}) collective-permute-start(f32[2,576,512]{2,1,0:T(8,128)S(1)} %pad_maximum_fusion.4), channel_id=1, source_target_pairs={{0,1},{1,0},{2,3},{3,2},{4,5},{5,4},{6,7},{7,6},{8,9},{9,8},{10,11... | collective-permute-start | bytes 7077896 | tf_op jit(solution)/shard_map/ppermute | solution.py:386
  (51 other events, 658.2 us)
Sparse Core Ops, SparseCore 0:
  169.7 90.6 all-gather.6
  320.0 114.8 all-gather.8
  620.5 78.8 all-gather.10

commit v2 on v1

--- a/solution.py
+++ b/solution.py
@@ -365,7 +365,9 @@
             input_output_aliases={5: 0} if len(operands) > 5 else {},
             compiler_params=pltpu.CompilerParams(vmem_limit_bytes=GRANT),
             cost_estimate=pl.CostEstimate(
-                flops=16 * m * n * BAND // parts, bytes_accessed=8 * m * n // parts, transcendentals=0
+                flops=(16 if parts == 1 else 1) * m * n * BAND // parts,
+                bytes_accessed=(8 if parts == 1 else 1) * m * n // parts,
+                transcendentals=0,
             ),
             name=name,
         )(*operands)
@@ -542,6 +544,7 @@
     y1, x1, mid1 = by_rows(first_kernel, "first", size, [at, raw1, image1, raw2, inv1], [F32, F32, square], 3)
     both = moves.sum_all(jnp.concatenate([mid1, moves.rows_at(x1, one)], axis=0))
     mid1, x1_head = both[:BAND], both[BAND:]
+    y1_r = moves.collect(after(y1, x1_head))
     tm1 = by_steps(transform_kernel, "transform", after(top1, x1), inv1)
     w1, pan2, w1_head, gram2, inner = by_rows(
         second_kernel,
@@ -555,38 +558,37 @@
     pan2_c = moves.along_row(placed2)
     both = moves.sum_all(after(jnp.concatenate([gram2, moves.rows_at(pan2, two)], axis=0), placed2))
     gram2, top2 = both[:BAND], both[BAND:]
-    inv2 = by_steps(factor_kernel, "factor", gram2)
-    both = moves.sum_all(after(jnp.concatenate([inner, moves.rows_at(w1, two)], axis=0), gram2))
+    raw3 = moves.deal(after(matrix[:, two : two + BAND], placed2))
+    ready = after(pan2_c, raw3)
+    high2, low2 = by_rows(halves_kernel, "halves", n, [col_at, ready], [BF16, BF16], 1)
+    both = moves.sum_all(after(jnp.concatenate([inner, moves.rows_at(w1, two)], axis=0), high2))
     inner, w1_next = both[: 2 * BAND], both[2 * BAND :]
-    pair1 = moves.collect(after(jnp.concatenate([y1, w1], axis=1), inner))
-    y1_r, w1_r = pair1[:, :BAND], pair1[:, BAND:]
-    raw3 = moves.deal(after(matrix[:, two : two + BAND], placed2))
-    ready = after(pan2_c, raw3, inv2)
-    high2, low2 = by_rows(halves_kernel, "halves", n, [col_at, ready], [BF16, BF16], 1)
+    w1_r = moves.collect(after(w1, high2))
     part2 = image_of(matrix, high2, low2)
+    inv2 = by_steps(factor_kernel, "factor", after(gram2, part2))
     image2 = moves.scatter_sum(part2)
-    y1_c, w1_c = by_rows(
-        sides_kernel, "sides", n, [col_at, raw1_c, raw2_c, after(pan2_c, part2), inv1, tm1, w1_head], [F32, F32], 3
-    )
-    tm2 = by_steps(transform_kernel, "transform", top2, inv2)
     x2, y2, mid2 = by_rows(
         next_kernel,
         "next",
         size,
-        [at, raw3, y1, w1, w1_next, low_head, inv1, image2, after(inner, tm2), pan2, inv2],
+        [at, raw3, y1, w1, w1_next, low_head, inv1, image2, inner, pan2, inv2],
         [F32, F32, square],
         8,
     )
     placed3 = moves.place(x2)
     x2_c = moves.along_row(placed3)
+    y1_c, w1_c = by_rows(
+        sides_kernel, "sides", n, [col_at, raw1_c, raw2_c, after(pan2_c, x2), inv1, tm1, w1_head], [F32, F32], 1
+    )
     mid2 = moves.sum_all(after(mid2, placed3))
+    pair2 = moves.collect(after(jnp.concatenate([y2, x2], axis=1), placed3))
+    y2_r, x2_r = pair2[:, :BAND], pair2[:, BAND:]
     half = update(matrix, y1_r, after(w1_r, x2), y1_c, w1_c, "update_first", 3)
+    tm2 = by_steps(transform_kernel, "transform", after(top2, half), inv2)
     (y2_c,) = by_rows(
         functools.partial(vectors_kernel, two), "vectors", n, [col_at, after(pan2_c, x2), inv2], [F32], 1
     )
-    (w2,) = by_rows(last_kernel, "last", size, [y2, x2, tm2, mid2], [F32], 2)
-    pair2 = moves.collect(jnp.concatenate([y2, w2], axis=1))
-    y2_r, w2_r = pair2[:, :BAND], pair2[:, BAND:]
+    (w2_r,) = by_rows(last_kernel, "last", m, [y2_r, x2_r, tm2, mid2], [F32], 2)
     (w2_c,) = by_rows(last_kernel, "last", n, [y2_c, x2_c, tm2, mid2], [F32], 2)
     updated = update(half, y2_r, w2_r, y2_c, w2_c, "update_second")
     return updated, jnp.concatenate([y1_r, y2_r], axis=1)

time: 798 us -> 792 us (level)
  waiting for transfers between devices: 181 us -> 173 us
    all_gather x3, waiting for transfers between devices: 0.01 us -> 15.7 us  [along_row(): lax.all_gather(piece, 'row', axis=0)]
    ppermute x30 -> x32, waiting for transfers between devices: 46.4 us -> 30.7 us  [over_col(): lax.ppermute(value, 'col', [(c, to(c)) for c in range(self.cols) if to(c)...]
    ppermute x14, waiting for transfers between devices: 71.7 us -> 63.7 us  [over_row(): return lax.ppermute(value, 'row', [(r, to(r)) for r in range(self.rows)])]
    ppermute x30 -> x32, starting transfers between devices: 90.7 us -> 83.2 us  [over_col(): lax.ppermute(value, 'col', [(c, to(c)) for c in range(self.cols) if to(c)...]
  transfers between devices with their start and end apart: 69 -> 71, of which waited for: 33 -> 27; matrix products, arithmetic and copies ran while one was open for 9% -> 9% of each run, Pallas kernels for 35% -> 36%
where the time goes in v2:
time: 792 us; the launch traced here: 782 us
  Pallas kernels  347 us (44%)
  waiting for transfers between devices  173 us (22%)
  starting transfers between devices  159 us (20%)
  local copies, waits for them, and re-layouts  44.3 us (6%)
  other arithmetic  44.2 us (6%)
  between operations  14.9 us (2%)
    pallas_call x16, Pallas kernels, by_steps(): pl.pallas_call(functools.partial(kernel, at), out_shape=jax.ShapeDtypeStr...  130 us
    pallas_call x4, Pallas kernels, update(): pl.pallas_call(update_kernel, grid=(each,), in_specs=specs, out_specs=pl....  102 us
    ppermute x32, starting transfers between devices, over_col(): lax.ppermute(value, 'col', [(c, to(c)) for c in range(self.cols) if to(c)...  83.2 us
    pallas_call x9, Pallas kernels, by_rows(): pl.pallas_call(kernel, grid=(rows // tile,), in_specs=in_specs, out_specs...  67.1 us
    ppermute x14, waiting for transfers between devices, over_row(): return lax.ppermute(value, 'row', [(r, to(r)) for r in range(self.rows)])  63.7 us
    pallas_call x2, Pallas kernels, image_of(): pl.pallas_call(image_kernel, grid=(n // deep,), in_specs=[pl.BlockSpec((m...  48.6 us
    ppermute x12, waiting for transfers between devices, line(): parts.append(lax.ppermute(parts[-1], 'row', pairs))  40.5 us
    ppermute x32, waiting for transfers between devices, over_col(): lax.ppermute(value, 'col', [(c, to(c)) for c in range(self.cols) if to(c)...  30.7 us
  transfers between devices with their start and end apart: 71, of which 27 were waited for; matrix products, arithmetic and copies ran while one was open for 9% of the time, Pallas kernels for 36%

profile of v2, /device:TPU:0, one launch (start us, length us, event | category | flops | bytes accessed | tf_op | source)
XLA Modules:
  0.0 782.2 jit_solution(1006959573529468324)
XLA Ops:
  36.3 8.2 %collective-permute-start.14 = (f32[288,256]{1,0:T(8,128)S(1)}, f32[288,256]{1,0:T(8,128)S(1)}, u32[]{:S(2)}, u32[]{:S(2)}) collective-permute-start(f32[288,256]{1,0:T(8,128)S(1)} %get-tuple-element.112), channel_id=1, source_target_pairs={{0,8},{4,12},{8,16},{12,20},{16,24},{20,28},{1,9},{5,13},{9,17},{1... | collective-permute-start | bytes 884744 | tf_op jit(solution)/shard_map/ppermute | solution.py:481
  106.7 15.1 %collective-permute-done.12 = f32[2,288,256]{2,1,0:T(8,128)S(1)} collective-permute-done((f32[2,288,256]{2,1,0:T(8,128)S(1)}, f32[2,288,256]{2,1,0:T(8,128)S(1)}, u32[]{:S(2)}, u32[]{:S(2)}) %collective-permute-start.12) | collective-permute-done | bytes 589856 | tf_op jit(solution)/shard_map/ppermute | solution.py:481
  123.4 10.2 %collective-permute-done.13 = f32[2,288,256]{2,1,0:T(8,128)S(1)} collective-permute-done((f32[2,288,256]{2,1,0:T(8,128)S(1)}, f32[2,288,256]{2,1,0:T(8,128)S(1)}, u32[]{:S(2)}, u32[]{:S(2)}) %collective-permute-start.13) | collective-permute-done | bytes 589856 | tf_op jit(solution)/shard_map/ppermute | solution.py:481
  136.9 8.5 %gram.1 = (f32[256,256]{1,0:T(8,128)}, bf16[4608,256]{1,0:T(8,128)(2,1)}, bf16[4608,256]{1,0:T(8,128)(2,1)}) custom-call(s32[1]{0:T(128)} %bitcast.1.offset_ref, f32[4608,256]{1,0:T(8,128)} %bitcast.131), custom_call_target="tpu_custom_call" | custom-call | flops 7247757312 | bytes 28311552 | tf_op jit(solution)/shard_map/gram/pallas_call | solution.py:266
  170.0 24.4 %image.2 = f32[2304,256]{1,0:T(8,128)} custom-call(f32[2304,4608]{1,0:T(8,128)} %matrix_ref.9, bf16[4608,256]{1,0:T(8,128)(2,1)} %get-tuple-element.39.high_ref, bf16[4608,256]{1,0:T(8,128)(2,1)} %get-tuple-element.40.low_ref), custom_call_target="tpu_custom_call" | custom-call | flops 21743271936 | bytes 42467328 | tf_op jit(solution)/shard_map/image/pallas_call | solution.py:305
  205.9 8.1 %factor.8.start_ref = f32[256,512]{1,0:T(8,128)} custom-call(f32[256,256]{1,0:T(8,128)} %add.173.start_ref), custom_call_target="tpu_custom_call" | custom-call | flops 6000000000 | bytes 4000000 | tf_op jit(solution)/shard_map/factor/pallas_call | solution.py:117
  214.1 8.2 %factor.9.start_ref = f32[256,512]{1,0:T(8,128)} custom-call(f32[256,512]{1,0:T(8,128)} %factor.8.start_ref), custom_call_target="tpu_custom_call" | custom-call | flops 6000000000 | bytes 4000000 | tf_op jit(solution)/shard_map/factor/pallas_call | solution.py:117
  225.2 8.1 %factor.10.start_ref = f32[256,512]{1,0:T(8,128)} custom-call(f32[256,512]{1,0:T(8,128)} %factor.9.start_ref), custom_call_target="tpu_custom_call" | custom-call | flops 6000000000 | bytes 4000000 | tf_op jit(solution)/shard_map/factor/pallas_call | solution.py:117
  261.0 8.5 %transform.8.refs_0_ = f32[256,512]{1,0:T(8,128)} custom-call(f32[256,256]{1,0:T(8,128)} %get-tuple-element.48.refs_0_.top_ref, f32[256,256]{1,0:T(8,128)} %factor.11.inv_ref.refs_1_), custom_call_target="tpu_custom_call" | custom-call | flops 6000000000 | bytes 4000000 | tf_op jit(solution)/shard_map/transform/pallas_call | solution.py:117
  276.6 8.1 %transform.9.refs_0_ = f32[256,512]{1,0:T(8,128)} custom-call(f32[256,512]{1,0:T(8,128)} %transform.8.refs_0_), custom_call_target="tpu_custom_call" | custom-call | flops 6000000000 | bytes 4000000 | tf_op jit(solution)/shard_map/transform/pallas_call | solution.py:117
  284.8 8.2 %transform.10.refs_0_ = f32[256,512]{1,0:T(8,128)} custom-call(f32[256,512]{1,0:T(8,128)} %transform.9.refs_0_), custom_call_target="tpu_custom_call" | custom-call | flops 6000000000 | bytes 4000000 | tf_op jit(solution)/shard_map/transform/pallas_call | solution.py:117
  321.3 18.6 %collective-permute-start.53 = (f32[256,256]{1,0:T(8,128)S(1)}, f32[256,256]{1,0:T(8,128)S(1)}, u32[]{:S(2)}, u32[]{:S(2)}) collective-permute-start(f32[256,256]{1,0:T(8,128)S(1)} %slice_select_fusion.1), channel_id=1, source_target_pairs={{0,1},{1,0},{2,3},{3,2},{4,5},{5,4},{6,7},{7,6},{8,9},{9,8},{10,11... | collective-permute-start | bytes 786440 | tf_op jit(solution)/shard_map/ppermute | solution.py:388
  339.9 9.4 %collective-permute-start.31 = (f32[576,256]{1,0:T(8,128)S(1)}, f32[576,256]{1,0:T(8,128)S(1)}, u32[]{:S(2)}, u32[]{:S(2)}) collective-permute-start(f32[576,256]{1,0:T(8,128)S(1)} %copy-done.10), channel_id=1, source_target_pairs={{0,2},{1,3},{2,0},{3,1},{4,6},{5,7},{6,4},{7,5},{8,10},{9,11},{10,... | collective-permute-start | bytes 1769480 | tf_op jit(solution)/shard_map/ppermute | solution.py:388
  350.9 18.0 %collective-permute-done.54 = f32[256,256]{1,0:T(8,128)S(1)} collective-permute-done((f32[256,256]{1,0:T(8,128)S(1)}, f32[256,256]{1,0:T(8,128)S(1)}, u32[]{:S(2)}, u32[]{:S(2)}) %collective-permute-start.54) | collective-permute-done | bytes 262176 | tf_op jit(solution)/shard_map/ppermute | solution.py:388
  377.5 9.0 %collective-permute-done.56 = f32[256,256]{1,0:T(8,128)S(1)} collective-permute-done((f32[256,256]{1,0:T(8,128)S(1)}, f32[256,256]{1,0:T(8,128)S(1)}, u32[]{:S(2)}, u32[]{:S(2)}) %collective-permute-start.56) | collective-permute-done | bytes 262176 | tf_op jit(solution)/shard_map/ppermute | solution.py:432
  388.0 28.7 %collective-permute-done.57 = f32[256,256]{1,0:T(8,128)S(1)} collective-permute-done((f32[256,256]{1,0:T(8,128)S(1)}, f32[256,256]{1,0:T(8,128)S(1)}, u32[]{:S(2)}, u32[]{:S(2)}) %collective-permute-start.57) | collective-permute-done | bytes 262176 | tf_op jit(solution)/shard_map/ppermute | solution.py:432
  419.2 15.7 %all-gather.9.cloned.1.call-done = f32[4608,256]{1,0:T(8,128)} async-done(((f32[576,256]{1,0:T(8,128)}), f32[4608,256]{1,0:T(8,128)}) %all-gather.9.cloned.1.call-update) | async-done | bytes 4718608 | tf_op jit(solution)/shard_map/all_gather | solution.py:515
  446.5 24.1 %image.3 = f32[2304,256]{1,0:T(8,128)} custom-call(f32[2304,4608]{1,0:T(8,128)} %matrix_ref.9, bf16[4608,256]{1,0:T(8,128)(2,1)} %get-tuple-element.53.high_ref, bf16[4608,256]{1,0:T(8,128)(2,1)} %get-tuple-element.57.low_ref), custom_call_target="tpu_custom_call" | custom-call | flops 21743271936 | bytes 42467328 | tf_op jit(solution)/shard_map/image/pallas_call | solution.py:305
  474.0 8.2 %factor.12.start_ref = f32[256,512]{1,0:T(8,128)} custom-call(f32[256,256]{1,0:T(8,128)} %get-tuple-element.60.start_ref), custom_call_target="tpu_custom_call" | custom-call | flops 6000000000 | bytes 4000000 | tf_op jit(solution)/shard_map/factor/pallas_call | solution.py:117
  482.8 8.1 %factor.13.start_ref = f32[256,512]{1,0:T(8,128)} custom-call(f32[256,512]{1,0:T(8,128)} %factor.12.start_ref), custom_call_target="tpu_custom_call" | custom-call | flops 6000000000 | bytes 4000000 | tf_op jit(solution)/shard_map/factor/pallas_call | solution.py:117
  494.9 8.2 %factor.14.start_ref = f32[256,512]{1,0:T(8,128)} custom-call(f32[256,512]{1,0:T(8,128)} %factor.13.start_ref), custom_call_target="tpu_custom_call" | custom-call | flops 6000000000 | bytes 4000000 | tf_op jit(solution)/shard_map/factor/pallas_call | solution.py:117
  522.4 8.5 %collective-permute-done.49 = f32[384,256]{1,0:T(8,128)S(1)} collective-permute-done((f32[384,256]{1,0:T(8,128)S(1)}, f32[384,256]{1,0:T(8,128)S(1)}, u32[]{:S(2)}, u32[]{:S(2)}) %collective-permute-start.49) | collective-permute-done | bytes 393248 | tf_op jit(solution)/shard_map/ppermute | solution.py:432
  553.2 14.0 %sides.1 = (f32[4608,256]{1,0:T(8,128)}, f32[4608,256]{1,0:T(8,128)}) custom-call(s32[1]{0:T(128)} %bitcast.1.offset_ref, f32[4608,256]{1,0:T(8,128)} %bitcast.134, f32[4608,256]{1,0:T(8,128)} %bitcast.136, f32[4608,256]{1,0:T(8,128)} %bitcast.138, f32[256,256]{1,0:T(8,128)} %factor.11.inv_ref.refs_1_, f32[256,256]{1,0:T(8,128)} %transform.11.tm_ref, ...), custom_call_target="tpu_custom_call" | custom-call | flops 3623878656 | bytes 28311552 | tf_op jit(solution)/shard_map/sides/pallas_call | solution.py:266
  567.3 19.5 %update_first.3.rest_0_ = f32[2304,4608]{1,0:T(8,128)} custom-call(f32[2304,4608]{1,0:T(8,128)} %matrix_ref.9, f32[2304,256]{1,0:T(8,128)} %bitcast.124, f32[2304,256]{1,0:T(8,128)} %bitcast.128, f32[4608,256]{1,0:T(8,128)} %get-tuple-element.65.yc_ref, f32[4608,256]{1,0:T(8,128)} %get-tuple-element.66.wc_ref), custom_call_target="tpu_custom_call" | custom-call | flops 905969664 | bytes 3538944 | tf_op jit(solution)/shard_map/update_first/pallas_call | solution.py:358
  587.0 24.5 %collective-permute-start.60 = (f32[576,512]{1,0:T(8,128)S(1)}, f32[576,512]{1,0:T(8,128)}, u32[]{:S(2)}, u32[]{:S(2)}) collective-permute-start(f32[576,512]{1,0:T(8,128)S(1)} %pad_maximum_fusion.7), channel_id=1, source_target_pairs={{0,2},{1,3},{2,0},{3,1},{4,6},{5,7},{6,4},{7,5},{8,10},{9,11},{10,... | collective-permute-start | bytes 3538952 | tf_op jit(solution)/shard_map/ppermute | solution.py:388
  611.6 19.4 %update_first.4.rest_0_ = f32[2304,4608]{1,0:T(8,128)} custom-call(f32[2304,4608]{1,0:T(8,128)} %matrix_ref.9, f32[2304,256]{1,0:T(8,128)} %bitcast.125, f32[2304,256]{1,0:T(8,128)} %bitcast.129, f32[4608,256]{1,0:T(8,128)} %get-tuple-element.65.yc_ref, f32[4608,256]{1,0:T(8,128)} %get-tuple-element.66.wc_ref, ...), custom_call_target="tpu_custom_call", output_to_operand_aliasing={{}: (5, {})} | custom-call | flops 905969664 | bytes 3538944 | tf_op jit(solution)/shard_map/update_first/pallas_call | solution.py:358
  630.9 19.5 %update_first.5.matrix_ref = f32[2304,4608]{1,0:T(8,128)} custom-call(f32[2304,4608]{1,0:T(8,128)} %matrix_ref.9, f32[2304,256]{1,0:T(8,128)} %bitcast.126, f32[2304,256]{1,0:T(8,128)} %bitcast.130, f32[4608,256]{1,0:T(8,128)} %get-tuple-element.65.yc_ref, f32[4608,256]{1,0:T(8,128)} %get-tuple-element.66.wc_ref, ...), custom_call_target="tpu_custom_call", output_to_operand_aliasing={{}: (5, {})} | custom-call | flops 905969664 | bytes 3538944 | tf_op jit(solution)/shard_map/update_first/pallas_call | solution.py:358
  651.2 8.5 %transform.12.refs_0_ = f32[256,512]{1,0:T(8,128)} custom-call(f32[256,256]{1,0:T(8,128)} %get-tuple-element.69.refs_0_, f32[256,256]{1,0:T(8,128)} %factor.15.new_ref.refs_1_.inv_ref), custom_call_target="tpu_custom_call" | custom-call | flops 6000000000 | bytes 4000000 | tf_op jit(solution)/shard_map/transform/pallas_call | solution.py:117
  664.7 8.1 %transform.13.refs_0_ = f32[256,512]{1,0:T(8,128)} custom-call(f32[256,512]{1,0:T(8,128)} %transform.12.refs_0_), custom_call_target="tpu_custom_call" | custom-call | flops 6000000000 | bytes 4000000 | tf_op jit(solution)/shard_map/transform/pallas_call | solution.py:117
  673.9 8.1 %transform.14.refs_0_ = f32[256,512]{1,0:T(8,128)} custom-call(f32[256,512]{1,0:T(8,128)} %transform.13.refs_0_), custom_call_target="tpu_custom_call" | custom-call | flops 6000000000 | bytes 4000000 | tf_op jit(solution)/shard_map/transform/pallas_call | solution.py:117
  721.9 9.9 %last.3.wc_ref = f32[4608,256]{1,0:T(8,128)} custom-call(f32[4608,256]{1,0:T(8,128)} %vectors.1.y_ref.yc_ref, f32[4608,256]{1,0:T(8,128)} %bitcast.147, f32[256,256]{1,0:T(8,128)} %transform.15.tm_ref, f32[256,256]{1,0:T(8,128)} %pad_maximum_fusion.12.mid_ref), custom_call_target="tpu_custom_call" | custom-call | flops 7247757312 | bytes 28311552 | tf_op jit(solution)/shard_map/last/pallas_call | solution.py:266
  731.8 43.7 %update_second.1 = f32[2304,4608]{1,0:T(8,128)} custom-call(f32[2304,4608]{1,0:T(8,128)} %update_first.5.matrix_ref, f32[2304,256]{1,0:T(8,128)} %get-tuple-element.79.y_ref.yr_ref, f32[2304,256]{1,0:T(8,128)} %last.2.wr_ref, f32[4608,256]{1,0:T(8,128)} %vectors.1.y_ref.yc_ref, f32[4608,256]{1,0:T(8,128)} %last.3.wc_ref), custom_call_target="tpu_custom_call" | custom-call | flops 43486543872 | bytes 84934656 | tf_op jit(solution)/shard_map/update_second/pallas_call | solution.py:358
  (278 shorter events, 320.1 us)
Async XLA Ops:
  7.2 299.6 %all-gather.7.cloned.1.call-start = ((), (), s32[]{:S(2)}) async-start(), calls=%async_computation | async-start | bytes 5308416 | tf_op jit(solution)/shard_map/all_gather | solution.py:515
  20.1 15.9 %collective-permute-start.1 = (f32[576,256]{1,0:T(8,128)S(1)}, f32[576,256]{1,0:T(8,128)S(1)}, u32[]{:S(2)}, u32[]{:S(2)}) collective-permute-start(f32[576,256]{1,0:T(8,128)S(1)} %get-tuple-element.74), channel_id=1, source_target_pairs={{0,8},{4,12},{8,9},{12,13},{16,10},{20,14},{24,11},{28,15}} | collective-permute-start | bytes 1769480 | tf_op jit(solution)/shard_map/ppermute | solution.py:392
  60.7 26.8 %collective-permute-start.4 = (f32[576,512]{1,0:T(8,128)S(1)}, f32[576,512]{1,0:T(8,128)S(1)}, u32[]{:S(2)}, u32[]{:S(2)}) collective-permute-start(f32[576,512]{1,0:T(8,128)S(1)} %get-tuple-element.84), channel_id=1, source_target_pairs={{0,3},{4,7},{8,11},{12,15},{16,19},{20,23},{24,27},{28,31}} | collective-permute-start | bytes 3538952 | tf_op jit(solution)/shard_map/ppermute | solution.py:388
  62.1 42.5 %collective-permute-start.5 = (f32[576,512]{1,0:T(8,128)S(1)}, f32[576,512]{1,0:T(8,128)S(1)}, u32[]{:S(2)}, u32[]{:S(2)}) collective-permute-start(f32[576,512]{1,0:T(8,128)S(1)} %get-tuple-element.83), channel_id=1, source_target_pairs={{0,2},{4,6},{8,10},{12,14},{16,18},{20,22},{24,26},{28,30}} | collective-permute-start | bytes 3538952 | tf_op jit(solution)/shard_map/ppermute | solution.py:388
  69.7 35.0 %collective-permute-start.6 = (f32[576,512]{1,0:T(8,128)S(1)}, f32[576,512]{1,0:T(8,128)S(1)}, u32[]{:S(2)}, u32[]{:S(2)}) collective-permute-start(f32[576,512]{1,0:T(8,128)S(1)} %get-tuple-element.82), channel_id=1, source_target_pairs={{0,1},{4,5},{8,9},{12,13},{16,17},{20,21},{24,25},{28,29}} | collective-permute-start | bytes 3538952 | tf_op jit(solution)/shard_map/ppermute | solution.py:388
  86.1 16.5 %collective-permute-start.11 = (f32[2,288,256]{2,1,0:T(8,128)S(1)}, f32[2,288,256]{2,1,0:T(8,128)S(1)}, u32[]{:S(2)}, u32[]{:S(2)}) collective-permute-start(f32[2,288,256]{2,1,0:T(8,128)S(1)} %pad_maximum_fusion.9), channel_id=1, source_target_pairs={{24,16},{28,20},{16,8},{20,12},{8,0},{12,4},{25,17},{29,21},{17,9}... | collective-permute-start | bytes 1769480 | tf_op jit(solution)/shard_map/ppermute | solution.py:481
  87.5 19.0 %collective-permute-start.20 = (f32[1,4,288,256]{3,2,0,1:T(8,128)S(1)}, f32[1,4,288,256]{3,2,0,1:T(8,128)S(1)}, u32[]{:S(2)}, u32[]{:S(2)}) collective-permute-start(f32[1,4,288,256]{3,2,0,1:T(8,128)S(1)} %dynamic-slice_bitcast_fusion.1), channel_id=1, source_target_pairs={{0,4},{4,0},{8,12},{12,8},{16,20},{20,16},{24,28},{28,24},{1,5},{5... | collective-permute-start | bytes 3538952 | tf_op jit(solution)/shard_map/ppermute | solution.py:432
  102.6 19.2 %collective-permute-start.12 = (f32[2,288,256]{2,1,0:T(8,128)S(1)}, f32[2,288,256]{2,1,0:T(8,128)S(1)}, u32[]{:S(2)}, u32[]{:S(2)}) collective-permute-start(f32[2,288,256]{2,1,0:T(8,128)S(1)} %collective-permute-done.11), channel_id=1, source_target_pairs={{16,8},{20,12},{8,0},{12,4},{17,9},{21,13},{9,1},{13,5},{18,10},{2... | collective-permute-start | bytes 1769480 | tf_op jit(solution)/shard_map/ppermute | solution.py:481
  103.9 19.2 %collective-permute-start.10 = (f32[2,288,256]{2,1,0:T(8,128)S(1)}, f32[2,288,256]{2,1,0:T(8,128)S(1)}, u32[]{:S(2)}, u32[]{:S(2)}) collective-permute-start(f32[2,288,256]{2,1,0:T(8,128)S(1)} %collective-permute-done.9), channel_id=1, source_target_pairs={{16,24},{20,28},{17,25},{21,29},{18,26},{22,30},{19,27},{23,31}} | collective-permute-start | bytes 1769480 | tf_op jit(solution)/shard_map/ppermute | solution.py:481
  157.2 41.0 %collective-permute-start.37 = (f32[512,256]{1,0:T(8,128)}, f32[512,256]{1,0:T(8,128)}, u32[]{:S(2)}, u32[]{:S(2)}) collective-permute-start(f32[512,256]{1,0:T(8,128)} %slice.165), channel_id=1, source_target_pairs={{0,2},{4,6},{8,10},{12,14},{16,18},{20,22},{24,26},{28,30}} | collective-permute-start | bytes 1572872 | tf_op jit(solution)/shard_map/ppermute | solution.py:388
  169.5 265.3 %all-gather.9.cloned.1.call-start = ((), (), s32[]{:S(2)}) async-start(), calls=%async_computation.1 | async-start | bytes 5308416 | tf_op jit(solution)/shard_map/all_gather | solution.py:515
  196.2 26.1 %collective-permute-start.21 = (f32[2,576,256]{2,1,0:T(8,128)S(1)}, f32[2,576,256]{2,1,0:T(8,128)}, u32[]{:S(2)}, u32[]{:S(2)}) collective-permute-start(f32[2,576,256]{2,1,0:T(8,128)S(1)} %select_bitcast_fusion.9), channel_id=1, source_target_pairs={{0,1},{1,0},{2,3},{3,2},{4,5},{5,4},{6,7},{7,6},{8,9},{9,8},{10,11... | collective-permute-start | bytes 3538952 | tf_op jit(solution)/shard_map/ppermute | solution.py:388
  200.1 49.8 %collective-permute-start.38 = (f32[512,256]{1,0:T(8,128)}, f32[512,256]{1,0:T(8,128)}, u32[]{:S(2)}, u32[]{:S(2)}) collective-permute-start(f32[512,256]{1,0:T(8,128)} %broadcast_select_fusion.2), channel_id=1, source_target_pairs={{0,1},{2,3},{4,5},{6,7},{8,9},{10,11},{12,13},{14,15},{16,17},{18,... | collective-permute-start | bytes 1572872 | tf_op jit(solution)/shard_map/ppermute | solution.py:388
  223.9 17.0 %collective-permute-start.22 = (f32[576,256]{1,0:T(8,128)S(1)}, f32[576,256]{1,0:T(8,128)S(1)}, u32[]{:S(2)}, u32[]{:S(2)}) collective-permute-start(f32[576,256]{1,0:T(8,128)S(1)} %select_bitcast_fusion.15), channel_id=1, source_target_pairs={{0,2},{1,3},{2,0},{3,1},{4,6},{5,7},{6,4},{7,5},{8,10},{9,11},{10,... | collective-permute-start | bytes 1769480 | tf_op jit(solution)/shard_map/ppermute | solution.py:388
  320.2 396.9 %all-gather.11.cloned.1.call-start = ((), (), s32[]{:S(2)}) async-start(), calls=%async_computation.2 | async-start | bytes 5308416 | tf_op jit(solution)/shard_map/all_gather | solution.py:515
  321.3 28.0 %collective-permute-start.53 = (f32[256,256]{1,0:T(8,128)S(1)}, f32[256,256]{1,0:T(8,128)S(1)}, u32[]{:S(2)}, u32[]{:S(2)}) collective-permute-start(f32[256,256]{1,0:T(8,128)S(1)} %slice_select_fusion.1), channel_id=1, source_target_pairs={{0,1},{1,0},{2,3},{3,2},{4,5},{5,4},{6,7},{7,6},{8,9},{9,8},{10,11... | collective-permute-start | bytes 786440 | tf_op jit(solution)/shard_map/ppermute | solution.py:388
  339.9 37.5 %collective-permute-start.31 = (f32[576,256]{1,0:T(8,128)S(1)}, f32[576,256]{1,0:T(8,128)S(1)}, u32[]{:S(2)}, u32[]{:S(2)}) collective-permute-start(f32[576,256]{1,0:T(8,128)S(1)} %copy-done.10), channel_id=1, source_target_pairs={{0,2},{1,3},{2,0},{3,1},{4,6},{5,7},{6,4},{7,5},{8,10},{9,11},{10,... | collective-permute-start | bytes 1769480 | tf_op jit(solution)/shard_map/ppermute | solution.py:388
  349.4 19.5 %collective-permute-start.54 = (f32[256,256]{1,0:T(8,128)S(1)}, f32[256,256]{1,0:T(8,128)S(1)}, u32[]{:S(2)}, u32[]{:S(2)}) collective-permute-start(f32[256,256]{1,0:T(8,128)S(1)} %select_add_fusion.1), channel_id=1, source_target_pairs={{0,2},{1,3},{2,0},{3,1},{4,6},{5,7},{6,4},{7,5},{8,10},{9,11},{10,... | collective-permute-start | bytes 786440 | tf_op jit(solution)/shard_map/ppermute | solution.py:388
  369.4 47.4 %collective-permute-start.40 = (f32[576,256]{1,0:T(8,128)S(1)}, f32[576,256]{1,0:T(8,128)S(1)}, u32[]{:S(2)}, u32[]{:S(2)}) collective-permute-start(f32[576,256]{1,0:T(8,128)S(1)} %get-tuple-element.91), channel_id=1, source_target_pairs={{0,3},{4,7},{8,11},{12,15},{16,19},{20,23},{24,27},{28,31}} | collective-permute-start | bytes 1769480 | tf_op jit(solution)/shard_map/ppermute | solution.py:388
  372.1 44.7 %collective-permute-start.41 = (f32[576,256]{1,0:T(8,128)S(1)}, f32[576,256]{1,0:T(8,128)S(1)}, u32[]{:S(2)}, u32[]{:S(2)}) collective-permute-start(f32[576,256]{1,0:T(8,128)S(1)} %get-tuple-element.90), channel_id=1, source_target_pairs={{0,2},{4,6},{8,10},{12,14},{16,18},{20,22},{24,26},{28,30}} | collective-permute-start | bytes 1769480 | tf_op jit(solution)/shard_map/ppermute | solution.py:388
  373.8 43.1 %collective-permute-start.42 = (f32[576,256]{1,0:T(8,128)S(1)}, f32[576,256]{1,0:T(8,128)S(1)}, u32[]{:S(2)}, u32[]{:S(2)}) collective-permute-start(f32[576,256]{1,0:T(8,128)S(1)} %get-tuple-element.89), channel_id=1, source_target_pairs={{0,1},{4,5},{8,9},{12,13},{16,17},{20,21},{24,25},{28,29}} | collective-permute-start | bytes 1769480 | tf_op jit(solution)/shard_map/ppermute | solution.py:388
  386.6 30.1 %collective-permute-start.57 = (f32[256,256]{1,0:T(8,128)S(1)}, f32[256,256]{1,0:T(8,128)S(1)}, u32[]{:S(2)}, u32[]{:S(2)}) collective-permute-start(f32[256,256]{1,0:T(8,128)S(1)} %add.196), channel_id=1, source_target_pairs={{0,16},{4,20},{8,24},{12,28},{16,0},{20,4},{24,8},{28,12},{1,17},{... | collective-permute-start | bytes 786440 | tf_op jit(solution)/shard_map/ppermute | solution.py:432
  387.9 160.1 %collective-permute-start.32 = (f32[2,576,256]{2,1,0:T(8,128)}, f32[2,576,256]{2,1,0:T(8,128)}, u32[]{:S(2)}, u32[]{:S(2)}) collective-permute-start(f32[2,576,256]{2,1,0:T(8,128)} %pad_maximum_fusion.5), channel_id=1, source_target_pairs={{0,1},{1,0},{2,3},{3,2},{4,5},{5,4},{6,7},{7,6},{8,9},{9,8},{10,11... | collective-permute-start | bytes 3538952 | tf_op jit(solution)/shard_map/ppermute | solution.py:388
  444.9 76.2 %collective-permute-start.43 = (f32[576,256]{1,0:T(8,128)}, f32[576,256]{1,0:T(8,128)}, u32[]{:S(2)}, u32[]{:S(2)}) collective-permute-start(f32[576,256]{1,0:T(8,128)} %get-tuple-element.54.w_ref), channel_id=1, source_target_pairs={{0,2},{1,3},{2,0},{3,1},{4,6},{5,7},{6,4},{7,5},{8,10},{9,11},{10,... | collective-permute-start | bytes 1769480 | tf_op jit(solution)/shard_map/ppermute | solution.py:388
  446.5 35.7 %collective-permute-start.45 = (f32[384,256]{1,0:T(8,128)S(1)}, f32[384,256]{1,0:T(8,128)S(1)}, u32[]{:S(2)}, u32[]{:S(2)}) collective-permute-start(f32[384,256]{1,0:T(8,128)S(1)} %slice_select_fusion), channel_id=1, source_target_pairs={{0,1},{1,0},{2,3},{3,2},{4,5},{5,4},{6,7},{7,6},{8,9},{9,8},{10,11... | collective-permute-start | bytes 1179656 | tf_op jit(solution)/shard_map/ppermute | solution.py:388
  473.5 30.3 %collective-permute-start.51 = (f32[2,576,256]{2,1,0:T(8,128)}, f32[2,576,256]{2,1,0:T(8,128)}, u32[]{:S(2)}, u32[]{:S(2)}) collective-permute-start(f32[2,576,256]{2,1,0:T(8,128)} %select_bitcast_fusion.4), channel_id=1, source_target_pairs={{0,1},{1,0},{2,3},{3,2},{4,5},{5,4},{6,7},{7,6},{8,9},{9,8},{10,11... | collective-permute-start | bytes 3538952 | tf_op jit(solution)/shard_map/ppermute | solution.py:388
  506.2 26.5 %collective-permute-start.52 = (f32[576,256]{1,0:T(8,128)}, f32[576,256]{1,0:T(8,128)}, u32[]{:S(2)}, u32[]{:S(2)}) collective-permute-start(f32[576,256]{1,0:T(8,128)} %select_bitcast_fusion.10), channel_id=1, source_target_pairs={{0,2},{1,3},{2,0},{3,1},{4,6},{5,7},{6,4},{7,5},{8,10},{9,11},{10,... | collective-permute-start | bytes 1769480 | tf_op jit(solution)/shard_map/ppermute | solution.py:388
  513.1 17.8 %collective-permute-start.49 = (f32[384,256]{1,0:T(8,128)S(1)}, f32[384,256]{1,0:T(8,128)S(1)}, u32[]{:S(2)}, u32[]{:S(2)}) collective-permute-start(f32[384,256]{1,0:T(8,128)S(1)} %add.189), channel_id=1, source_target_pairs={{0,16},{4,20},{8,24},{12,28},{16,0},{20,4},{24,8},{28,12},{1,17},{... | collective-permute-start | bytes 1179656 | tf_op jit(solution)/shard_map/ppermute | solution.py:432
  532.2 15.8 %collective-permute-start.44 = (f32[2,576,256]{2,1,0:T(8,128)}, f32[2,576,256]{2,1,0:T(8,128)S(1)}, u32[]{:S(2)}, u32[]{:S(2)}) collective-permute-start(f32[2,576,256]{2,1,0:T(8,128)} %pad_maximum_fusion.6), channel_id=1, source_target_pairs={{0,1},{1,0},{2,3},{3,2},{4,5},{5,4},{6,7},{7,6},{8,9},{9,8},{10,11... | collective-permute-start | bytes 3538952 | tf_op jit(solution)/shard_map/ppermute | solution.py:388
  587.0 74.5 %collective-permute-start.60 = (f32[576,512]{1,0:T(8,128)S(1)}, f32[576,512]{1,0:T(8,128)}, u32[]{:S(2)}, u32[]{:S(2)}) collective-permute-start(f32[576,512]{1,0:T(8,128)S(1)} %pad_maximum_fusion.7), channel_id=1, source_target_pairs={{0,2},{1,3},{2,0},{3,1},{4,6},{5,7},{6,4},{7,5},{8,10},{9,11},{10,... | collective-permute-start | bytes 3538952 | tf_op jit(solution)/shard_map/ppermute | solution.py:388
  611.5 39.0 %collective-permute-start.62 = (f32[128,256]{1,0:T(8,128)S(1)}, f32[128,256]{1,0:T(8,128)S(1)}, u32[]{:S(2)}, u32[]{:S(2)}) collective-permute-start(f32[128,256]{1,0:T(8,128)S(1)} %slice_select_fusion.2), channel_id=1, source_target_pairs={{0,1},{1,0},{2,3},{3,2},{4,5},{5,4},{6,7},{7,6},{8,9},{9,8},{10,11... | collective-permute-start | bytes 393224 | tf_op jit(solution)/shard_map/ppermute | solution.py:388
  664.6 35.8 %collective-permute-start.61 = (f32[2,576,512]{2,1,0:T(8,128)}, f32[2,576,512]{2,1,0:T(8,128)}, u32[]{:S(2)}, u32[]{:S(2)}) collective-permute-start(f32[2,576,512]{2,1,0:T(8,128)} %pad_maximum_fusion.4), channel_id=1, source_target_pairs={{0,1},{1,0},{2,3},{3,2},{4,5},{5,4},{6,7},{7,6},{8,9},{9,8},{10,11... | collective-permute-start | bytes 7077896 | tf_op jit(solution)/shard_map/ppermute | solution.py:388
  (56 other events, 638.8 us)
Sparse Core Ops, SparseCore 0:
  169.6 90.2 all-gather.6
  320.3 114.4 all-gather.8
  548.1 101.8 all-gather.10
